TPU v7x, 32 devices: a whole 2x2x4 slice. The times are simulated.
32 devices in a mesh: seq: 8 (over y, x, core), head: 4 (over z).
Axes of the slice: x: 2, y: 2, z: 4, core: 2. Of those that a mesh axis runs over, the one named last changes fastest.
Arguments:
- ssd_input: bfloat16 [2048, 8192], P('seq', 'head'), may hold values from -6 to 6
- gate_input: bfloat16 [2048, 8192], P('seq', 'head'), may hold values from -6 to 6
- write_vectors: bfloat16 [2048, 2048], P('seq', 'head'), may hold values from -1 to 1
- read_vectors: bfloat16 [2048, 2048], P('seq', 'head'), may hold values from -6 to 6
- log_decay: float32 [2048, 128], P('seq', 'head'), may hold values from -1 to 0
- skip_gain: float32 [128], P('head'), may hold values from 0.5 to 1.5
- norm_gain: float32 [8192], P('head'), may hold values from 0.5 to 1.5
- out_weight: bfloat16 [8192, 8192], P(None, 'head'), may hold values from -0.0625 to 0.0625
- out_grad: bfloat16 [2048, 8192], P('seq', 'head'), may hold values from -6 to 6
Outputs:
- layer_out: bfloat16 [2048, 8192], P('seq', 'head')
- input_grad: bfloat16 [2048, 8192], P('seq', 'head')
- gate_grad: bfloat16 [2048, 8192], P('seq', 'head')
- write_grad: bfloat16 [2048, 2048], P('seq', 'head')
- read_grad: bfloat16 [2048, 2048], P('seq', 'head')
- decay_grad: float32 [2048, 128], P('seq', 'head')
- weight_grad: bfloat16 [8192, 8192], P('seq', 'head')
All inputs are finite; a program needn't handle non-finite values.
Results may differ from a plain program's by a relative error of at most 0.018.
Values may be sent and summed in bfloat16 or wider, within the bound.
A program may use at most 192 MiB of HBM per device.

v0:
```python
from functools import partial

import jax
import jax.numpy as jnp
from jax import lax
from jax.sharding import PartitionSpec as P

HALF_HEADS = 128
P_SIZE = 64
N = 256
G = 8
SPAN = 256


epsilon = 1e-05
highest = lax.Precision.HIGHEST


def entering(x, axis, join, neutral):
    place = lax.axis_index(axis)
    gathered = jax.tree.map(
        lambda a, kind: lax.all_gather(a.astype(kind), axis), x, (jnp.bfloat16, jnp.bfloat16)
    )
    state = jax.tree.map(lambda a, e: jnp.zeros_like(a) + jnp.asarray(e, a.dtype), x, neutral)

    def entering_one(hop, state):
        return join(
            state,
            jax.tree.map(
                lambda a, own: lax.dynamic_index_in_dim(a, hop, 0, False).astype(own.dtype),
                gathered,
                x,
            ),
        )

    return lax.fori_loop(0, place, entering_one, state)


def prefix(x, axis, join, neutral):
    count = lax.axis_size(axis)
    place = lax.axis_index(axis)
    ahead = count - 1 - place
    gathered = jax.tree.map(
        lambda a, kind: lax.all_gather(a.astype(kind), axis),
        x,
        jax.tree.map(lambda a: jnp.bfloat16 if a.dtype == jnp.float32 else a.dtype, x),
    )
    state = jax.tree.map(lambda a, e: jnp.zeros_like(a) + jnp.asarray(e, a.dtype), x, neutral)

    def prefix_one(hop, state):
        source = count - 1 - hop
        return join(
            state,
            jax.tree.map(
                lambda a, own: lax.dynamic_index_in_dim(a, source, 0, False).astype(own.dtype),
                gathered,
                x,
            ),
        )

    return lax.fori_loop(0, ahead, prefix_one, state)


def block_scan(state_now, pieces):
    input_block, write_block, read_block, decay_block = pieces
    row_count = decay_block.shape[0]
    group_count, per_group = (state_now.shape[0], state_now.shape[1])
    input_heads = input_block.reshape(row_count, group_count, per_group, P_SIZE)
    write_heads = write_block.reshape(row_count, group_count, N)
    read_heads = read_block.reshape(row_count, group_count, N)
    cumulative = jnp.cumsum(decay_block, axis=0).reshape(row_count, group_count, per_group)
    by_head = jnp.transpose(cumulative, (1, 2, 0))
    causal = lax.broadcasted_iota(jnp.int32, (row_count, row_count), 0) >= lax.broadcasted_iota(
        jnp.int32, (row_count, row_count), 1
    )
    gap_table = jnp.where(causal, by_head[..., :, None] - by_head[..., None, :], 0.0)
    decay_table = jnp.where(causal, jnp.exp(gap_table), 0.0)
    scores = jnp.einsum("tgn,sgn->gts", read_heads, write_heads, precision=highest)
    weights = scores[:, None] * decay_table
    inner_sum = jnp.einsum("gkts,sgkp->tgkp", weights, input_heads, precision=highest)
    carried = jnp.einsum("tgn,gkpn->tgkp", read_heads, state_now, precision=highest)
    output = inner_sum + jnp.exp(cumulative)[..., None] * carried
    final_log = cumulative[-1]
    weighted = input_heads * jnp.exp(final_log[None] - cumulative)[..., None]
    fresh_state = jnp.einsum("sgkp,sgn->gkpn", weighted, write_heads, precision=highest)
    next_state = jnp.exp(final_log)[..., None, None] * state_now + fresh_state
    return (next_state, output.reshape(row_count, group_count * per_group * P_SIZE))


def block_end(state_now, pieces):
    input_block, write_block, decay_block = pieces
    row_count = decay_block.shape[0]
    group_count, per_group = (state_now.shape[0], state_now.shape[1])
    input_heads = input_block.reshape(row_count, group_count, per_group, P_SIZE)
    write_heads = write_block.reshape(row_count, group_count, N)
    cumulative = jnp.cumsum(decay_block, axis=0).reshape(row_count, group_count, per_group)
    final_log = cumulative[-1]
    weighted = input_heads * jnp.exp(final_log[None] - cumulative)[..., None]
    fresh_state = jnp.einsum("sgkp,sgn->gkpn", weighted, write_heads, precision=highest)
    return (jnp.exp(final_log)[..., None, None] * state_now + fresh_state, None)


def in_blocks(operand):
    return operand.reshape(operand.shape[0] // SPAN, SPAN, operand.shape[1])


def ssd_run(inputs, writes, reading, decays, start_state):
    row_count = decays.shape[0]
    final_state, outputs = lax.scan(
        block_scan,
        start_state,
        (in_blocks(inputs), in_blocks(writes), in_blocks(reading), in_blocks(decays)),
    )
    return (outputs.reshape(row_count, outputs.shape[2]), final_state)


def gate_norm(ssd_out, inputs, gate_values, skip_gain, norm_gain):
    row_count = ssd_out.shape[0]
    head_count = skip_gain.shape[0]
    direct = (inputs.reshape(row_count, head_count, P_SIZE) * skip_gain[:, None]).reshape(
        row_count, head_count * P_SIZE
    )
    gated_vals = (ssd_out + direct) * jax.nn.silu(gate_values)
    grouped = gated_vals.reshape(row_count, -1, HALF_HEADS * P_SIZE // G)
    factor = lax.rsqrt(jnp.mean(grouped * grouped, axis=2, keepdims=True) + epsilon)
    return (grouped * factor).reshape(row_count, head_count * P_SIZE) * norm_gain


def combine(earlier, later):
    return (earlier[0] * later[0], later[0][..., None, None] * earlier[1] + later[1])


def per_device(
    ssd_input,
    gate_input,
    write_vectors,
    read_vectors,
    log_decay,
    skip_gain,
    norm_gain,
    out_weight,
    out_grad,
):
    row_count, head_count = log_decay.shape
    group_count = write_vectors.shape[1] // N
    per_group = head_count // group_count
    inputs = ssd_input.astype(jnp.float32)
    gate_values = gate_input.astype(jnp.float32)
    writes = write_vectors.astype(jnp.float32)
    reading = read_vectors.astype(jnp.float32)
    zero_state = jnp.zeros((group_count, per_group, P_SIZE, N), jnp.float32)
    own_state, unused = lax.scan(
        block_end, zero_state, (in_blocks(inputs), in_blocks(writes), in_blocks(log_decay))
    )
    cumulative = jnp.cumsum(log_decay, axis=0)
    own_decay = jnp.exp(cumulative[-1]).reshape(group_count, per_group)
    identity_pair = (jnp.ones_like(own_decay), zero_state)
    decay_before, start_state = entering((own_decay, own_state), "seq", combine, identity_pair)
    (ssd_out, end_state), ssd_pull = jax.vjp(
        ssd_run, inputs, writes, reading, log_decay, start_state
    )
    norm_fn = partial(gate_norm, skip_gain=skip_gain, norm_gain=norm_gain)
    normed, norm_pull = jax.vjp(norm_fn, ssd_out, inputs, gate_values)
    normed_half = normed.astype(jnp.bfloat16)
    partial_out = jnp.einsum(
        "th,dh->td", normed_half, out_weight, preferred_element_type=jnp.float32
    )
    layer_out = lax.psum_scatter(
        partial_out.astype(jnp.bfloat16), "head", scatter_dimension=1, tiled=True
    )
    full_grad = lax.all_gather(out_grad, "head", axis=1, tiled=True)
    normed_grad = jnp.dot(full_grad, out_weight, preferred_element_type=jnp.float32)
    ssd_grad, skip_input_grad, gate_grad = norm_pull(normed_grad)
    scaled_grad = ssd_grad.reshape(row_count, group_count, per_group, P_SIZE) * jnp.exp(
        cumulative
    ).reshape(row_count, group_count, per_group, 1)
    state_direct = jnp.einsum(
        "tgkp,tgn->gkpn", scaled_grad, reading.reshape(row_count, group_count, N), precision=highest
    )
    decay_after, end_grad = prefix((own_decay, state_direct), "seq", combine, identity_pair)
    input_part, write_grad, read_grad, decay_grad, start_grad = ssd_pull((ssd_grad, end_grad))
    input_grad = skip_input_grad + input_part
    weight_grad = lax.psum_scatter(
        jnp.einsum("td,th->dh", full_grad, normed_half, preferred_element_type=jnp.float32).astype(
            jnp.bfloat16
        ),
        "seq",
        scatter_dimension=0,
        tiled=True,
    )
    return (
        layer_out,
        input_grad.astype(jnp.bfloat16),
        gate_grad.astype(jnp.bfloat16),
        write_grad.astype(jnp.bfloat16),
        read_grad.astype(jnp.bfloat16),
        decay_grad,
        weight_grad,
    )


def solution(mesh):
    in_specs = (
        P("seq", "head"),
        P("seq", "head"),
        P("seq", "head"),
        P("seq", "head"),
        P("seq", "head"),
        P("head"),
        P("head"),
        P(None, "head"),
        P("seq", "head"),
    )
    out_specs = (
        P("seq", "head"),
        P("seq", "head"),
        P("seq", "head"),
        P("seq", "head"),
        P("seq", "head"),
        P("seq", "head"),
        P("seq", "head"),
    )
    return jax.shard_map(
        per_device, mesh=mesh, in_specs=in_specs, out_specs=out_specs, check_vma=False
    )
```

profile of v0, /device:TPU:0, one launch (start us, length us, event | category | flops | bytes accessed | tf_op | source)
XLA Modules:
  0.0 558.5 jit_solution(12330357056432590875)
XLA Ops:
  18.2 10.2 %all_gather.21 = bf16[8,2,16]{2,1,0:T(2,128)(2,1)S(1)} all-gather(bf16[1,2,16]{2,1,0:T(2,128)(2,1)S(1)} %convert_element_type.101), channel_id=1, replica_groups=mesh['seq'=8,'head'=4] {'seq'}, dimensions={0}, use_global_device_ids=true | all-gather | bytes 576 | tf_op jit(solution)/shard_map/all_gather | solution.py:22
  30.2 42.0 %all-gather.8.cloned.1.call-done = bf16[16,16,64,256]{3,2,1,0:T(8,128)(2,1)} async-done(((bf16[2,16,64,256]{3,2,1,0:T(8,128)(2,1)}), bf16[16,16,64,256]{3,2,1,0:T(8,128)(2,1)}) %all-gather.8.cloned.1.call-update) | async-done | bytes 8388624 | tf_op jit(solution)/shard_map/all_gather | solution.py:22
  75.3 8.4 %fusion.27 = f32[256,2,16,64]{0,3,2,1:T(8,128)} fusion(f32[2,16,64,256]{3,2,1,0:T(8,128)S(1)} %fusion.61, bf16[256,2,16,64]{0,3,2,1:T(8,128)(2,1)S(1)} %bitcast.181, f32[2,16,256]{2,1,0:T(8,128)S(1)} %bitcast.186, f32[2,256,256]{2,1,0:T(8,128)S(1)} %copy-done.26, pred[256,256]{1,0:T(8,128)(4,1)S(1)} %copy-done.33, f32[256,2,16]{0,2,1:T(8,128)S(1)} %copy.143), kind=kOutput, calls=%fused_computation.45 | convolution fusion | flops 1620049920 | bytes 5898240 | tf_op jit(solution)/shard_map/jvp()/while/body/eval_jaxpr/gkts,sgkp->tgkp/dot_general | solution.py:80
  86.7 67.9 %all-gather.6.cloned.1.call-done = bf16[256,8192]{1,0:T(8,128)(2,1)} async-done(((bf16[256,2048]{1,0:T(8,128)(2,1)}), bf16[256,8192]{1,0:T(8,128)(2,1)}) %all-gather.6.cloned.1.call-update) | async-done | bytes 4194320 | tf_op jit(solution)/shard_map/all_gather | solution.py:171
  154.6 19.0 %fusion.72 = (f32[256,2048]{1,0:T(8,128)}, f32[256,2048]{1,0:T(8,128)}, f32[256,2048]{1,0:T(8,128)}) fusion(bf16[256,2048]{1,0:T(8,128)(2,1)} %param.14, f32[256,2048]{1,0:T(8,128)} %copy.149, f32[2048]{0:T(1024)S(1)} %mul.389, bf16[256,2048]{1,0:T(8,128)(2,1)S(1)} %copy-done.5, f32[2048]{0:T(1024)} %param.19, ...), kind=kOutput, calls=%fused_computation.104 | convolution fusion | flops 8596226048 | bytes 48250880 | tf_op jit(solution)/shard_map/dot_general | solution.py:172
  173.7 4.0 mul.404
  182.1 4.1 mul.395
  210.3 16.4 %convert_bitcast_fusion = bf16[8192,2048]{0,1:T(8,128)(2,1)} fusion(bf16[256,2048]{1,0:T(8,128)(2,1)S(1)} %copy-done.8, bf16[256,8192]{1,0:T(8,128)(2,1)} %all-gather.6.cloned.1.call-done), kind=kOutput, calls=%fused_computation.4 | convolution fusion | flops 8606711808 | bytes 38797312 | tf_op jit(solution)/shard_map/td,th->dh/dot_general | solution.py:184
  226.8 18.2 %convolution_convert_fusion = bf16[256,8192]{1,0:T(8,128)(2,1)} fusion(bf16[256,2048]{1,0:T(8,128)(2,1)S(1)} %copy-done.8, bf16[8192,2048]{1,0:T(8,128)(2,1)} %param.20), kind=kOutput, calls=%fused_computation.5 | convolution fusion | flops 8592031744 | bytes 38797312 | tf_op jit(solution)/shard_map/th,dh->td/dot_general | solution.py:165
  246.2 10.3 %fusion.7 = (f32[2,16,256]{2,1,0:T(8,128)}, f32[2,16,256]{2,1,0:T(8,128)}, f32[2,256,256]{2,1,0:T(8,128)S(1)}) fusion(f32[2,16,256]{2,1,0:T(8,128)S(1)} %bitcast.187, f32[2,256,256]{2,1,0:T(8,128)S(1)} %copy-done.27, pred[256,256]{1,0:T(8,128)(4,1)} %iota_compare_fusion, f32[2,16,64,256]{3,2,1,0:T(8,128)} %bitcast.161, bf16[256,2,16,64]{0,3,2,1:T(8,128)(2,1)} %bitcast.180), kind=kOutput, calls=%fused_computation.14 | convolution fusion | flops 1633533952 | bytes 4358144 | tf_op jit(solution)/shard_map/transpose(jvp())/while/body/eval_jaxpr/gkts,sgkp->tgkp/dot_general | solution.py:80
  262.5 5.1 fusion.48
  272.2 28.0 %while.21 = (s32[]{:T(128)}, f32[2,16,64,256]{3,2,1,0:T(8,128)}, s32[]{:T(128)}, bf16[8,2,16]{2,1,0:T(2,128)(2,1)S(1)}, bf16[8,2,16,64,256]{4,3,2,1,0:T(8,128)(2...) while((s32[]{:T(128)}, f32[2,16,64,256]{3,2,1,0:T(8,128)}, s32[]{:T(128)}, ...), condition=%wide.region_8.9_spmd, body=%wide.region_7.8_spmd.sunk | while | flops 1572902 | bytes 5243355 | solution.py:61
  275.7 4.1 convert_add_fusion.5
  279.8 4.1 convert_add_fusion.5
  283.9 4.1 convert_add_fusion.5
  288.0 4.0 convert_add_fusion.5
  292.0 4.0 convert_add_fusion.5
  296.0 4.0 convert_add_fusion.5
  300.3 4.4 fusion.26
  304.7 8.5 %bitcast_add_fusion = f32[256,2,16,64]{0,3,2,1:T(8,128)} fusion(f32[2,16,64,256]{3,2,1,0:T(8,128)S(1)} %get-tuple-element.545, f32[2,16,64,256]{3,2,1,0:T(8,128)S(1)} %bitcast.163, f32[2,16,256]{2,1,0:T(8,128)S(1)} %bitcast.188, f32[2,256,256]{2,1,0:T(8,128)S(1)} %copy-done.28, pred[256,256]{1,0:T(8,128)(4,1)S(1)} %copy-done.34, f32[256,2,16]{0,2,1:T(8,128)S(1)} %copy.146), kind=kOutput, calls=%fused_computation.39 | convolution fusion | flops 1620049920 | bytes 6946816 | tf_op jit(solution)/shard_map/transpose(jvp())/while/body/eval_jaxpr/gkts,sgkp->tgkp/dot_general | solution.py:80
  316.5 5.8 %fusion.45 = f32[256,2,256]{0,2,1:T(8,128)S(1)} fusion(f32[2,16,64,256]{3,2,1,0:T(8,128)} %get-tuple-element.464, f32[256,2,16,64]{0,3,2,1:T(8,128)} %bitcast.159, f32[256,2,16]{0,2,1:T(8,128)S(1)} %copy.146), kind=kOutput, calls=%fused_computation.60 | convolution fusion | flops 1611137024 | bytes 4751360 | tf_op jit(solution)/shard_map/transpose(jvp())/while/body/eval_jaxpr/sgkp,sgn->gkpn/dot_general | solution.py:85
  333.7 138.3 %reduce-scatter.5.cloned.1.call-done = bf16[1024,2048]{0,1:T(8,128)(2,1)} async-done(((bf16[8192,2048]{0,1:T(8,128)(2,1)}), bf16[1024,2048]{0,1:T(8,128)(2,1)}) %reduce-scatter.5.cloned.1.call-update) | async-done | bytes 4194320 | tf_op jit(solution)/shard_map/reduce_scatter | solution.py:183
  472.1 6.4 %copy.169 = bf16[1024,2048]{1,0:T(8,128)(2,1)} copy(bf16[1024,2048]{0,1:T(8,128)(2,1)} %reduce-scatter.5.cloned.1.call-done) | data formatting | bytes 8388608
  478.5 73.2 %reduce-scatter.3.cloned.1.call-done = bf16[256,2048]{1,0:T(8,128)(2,1)} async-done(((bf16[256,8192]{1,0:T(8,128)(2,1)}), bf16[256,2048]{1,0:T(8,128)(2,1)}) %reduce-scatter.3.cloned.1.call-update) | async-done | bytes 1048592 | tf_op jit(solution)/shard_map/reduce_scatter | solution.py:168
  (173 shorter events, 76.9 us)
Async XLA Ops:
  7.2 5.1 copy-start.5
  7.2 65.1 %all-gather.8.cloned.1.call-start = ((), (), s32[]{:S(2)}) async-start(), calls=%async_computation.5 | async-start | bytes 9437184 | tf_op jit(solution)/shard_map/all_gather | solution.py:22
  15.1 139.6 %all-gather.6.cloned.1.call-start = ((), (), s32[]{:S(2)}) async-start(), calls=%async_computation.3 | async-start | bytes 5242880 | tf_op jit(solution)/shard_map/all_gather | solution.py:171
  15.8 254.8 %all-gather.10.cloned.1.call-start = ((), (), s32[]{:S(2)}) async-start(), calls=%async_computation.6 | async-start | bytes 9437184 | tf_op jit(solution)/shard_map/all_gather | solution.py:44
  16.0 14.2 %copy-start.16 = (bf16[256,2,256]{0,2,1:T(8,128)(2,1)}, bf16[256,2,256]{0,2,1:T(8,128)(2,1)S(1)}, u32[]{:S(2)}) copy-start(bf16[256,2,256]{0,2,1:T(8,128)(2,1)S(1)} %copy.159) | copy-start | bytes 786436
  17.7 54.6 %copy-start.9 = (bf16[256,2,256]{2,1,0:T(2,128)(2,1)}, bf16[256,2,256]{2,1,0:T(2,128)(2,1)S(1)}, u32[]{:S(2)}) copy-start(bf16[256,2,256]{2,1,0:T(2,128)(2,1)S(1)} %reshape.506) | copy-start | bytes 786436
  17.9 54.4 %copy-start.14 = (bf16[256,2,256]{0,2,1:T(8,128)(2,1)}, bf16[256,2,256]{0,2,1:T(8,128)(2,1)S(1)}, u32[]{:S(2)}) copy-start(bf16[256,2,256]{0,2,1:T(8,128)(2,1)S(1)} %copy.158) | copy-start | bytes 786436
  75.3 8.4 %copy-start.6 = (f32[2,16,64,256]{3,2,1,0:T(8,128)}, f32[2,16,64,256]{3,2,1,0:T(8,128)S(1)}, u32[]{:S(2)}) copy-start(f32[2,16,64,256]{3,2,1,0:T(8,128)S(1)} %fusion.61) | copy-start | bytes 6291460
  206.4 3.9 copy-start.8
  210.3 261.8 %reduce-scatter.5.cloned.1.call-start = ((), (), s32[]{:S(2)}) async-start(), calls=%async_computation.4 | async-start | bytes 37748736 | tf_op jit(solution)/shard_map/reduce_scatter | solution.py:183
  226.8 324.9 %reduce-scatter.3.cloned.1.call-start = ((), (), s32[]{:S(2)}) async-start(), calls=%async_computation.2 | async-start | bytes 5242880 | tf_op jit(solution)/shard_map/reduce_scatter | solution.py:168
  258.1 3.6 copy-start.35
  262.5 5.1 copy-start.17
  300.2 4.4 copy-start.3
  300.2 4.4 copy-start.28
  300.2 4.4 copy-start.34
  316.5 5.8 %copy-start.15 = (bf16[256,2,256]{0,2,1:T(8,128)(2,1)S(1)}, bf16[256,2,256]{0,2,1:T(8,128)(2,1)}, u32[]{:S(2)}) copy-start(bf16[256,2,256]{0,2,1:T(8,128)(2,1)} %copy-done.14) | copy-start | bytes 786436
  324.1 2.5 copy-start.11
  324.1 2.5 copy-start.13
  324.1 2.5 copy-start.20
  324.1 2.5 copy-start.21
  324.1 2.5 copy-start.22
  326.6 4.0 copy-start.4
  472.1 79.6 %copy-start.1 = (f32[256,32]{0,1:T(8,128)S(1)}, f32[256,32]{0,1:T(8,128)}, u32[]{:S(2)}) copy-start(f32[256,32]{0,1:T(8,128)} %param.17) | copy-start | bytes 98308
  (23 other events, 37.6 us)
Sparse Core Ops, SparseCore 0:
  15.2 57.0 all-gather.7
  73.8 80.7 all-gather.5
  210.4 52.9 all-gather.9
  266.8 205.2 reduce-scatter.4
  474.9 76.7 reduce-scatter.2
where the time goes:
time: 563 us; the launch traced here: 558 us
  waiting for transfers between devices  322 us (57%)
  matrix products  107 us (19%)
  other arithmetic  52.4 us (9%)
  local copies, waits for them, and re-layouts  51 us (9%)
  between operations  14.7 us (3%)
  blocking collectives  10.2 us (2%)
    reduce_scatter x1, waiting for transfers between devices, per_device(): lax.psum_scatter(jnp.einsum('td,th->dh', full_grad, normed_half, preferre...  138 us
    reduce_scatter x1, waiting for transfers between devices, per_device(): lax.psum_scatter(partial_out.astype(jnp.bfloat16), 'head', scatter_dimens...  73.2 us
    all_gather x1, waiting for transfers between devices, per_device(): full_grad = lax.all_gather(out_grad, 'head', axis=1, tiled=True)  67.9 us
    all_gather x1, waiting for transfers between devices, entering(): lax.all_gather(a.astype(kind), axis)  42 us
    add x7, other arithmetic, combine(): later[0][..., None, None] * earlier[1] + later[1]  27.8 us
    dot_general x3, matrix products, block_scan(): jnp.einsum('gkts,sgkp->tgkp', weights, input_heads, precision=highest)  27.2 us
    dot_general x1, matrix products, per_device(): jnp.dot(full_grad, out_weight, preferred_element_type=jnp.float32)  19 us
    dot_general x1, matrix products, per_device(): jnp.einsum('th,dh->td', normed_half, out_weight, preferred_element_type=j...  18.2 us
  transfers between devices with their start and end apart: 5, of which 4 were waited for; matrix products, arithmetic and copies ran while one was open for 26% of the time, Pallas kernels for 0%

commit v1 on v0

v1 whole, which is shorter than its diff:
```python
from functools import partial

import jax
import jax.numpy as jnp
from jax import lax
from jax.experimental import pallas as pl
from jax.experimental.pallas import tpu as pltpu
from jax.sharding import PartitionSpec as P

P_SIZE = 64
N = 256
PAIR = 2 * P_SIZE

epsilon = 1e-05
highest = lax.Precision.HIGHEST
f32 = jnp.float32
bf16 = jnp.bfloat16
VMEM_LIMIT = 56 * 1024 * 1024


def dot(a, b, ca, cb, precision=None):
    return lax.dot_general(
        a, b, (((ca,), (cb,)), ((), ())), preferred_element_type=f32, precision=precision
    )


def spread(col, j, left):
    return jnp.where(left, col[:, 2 * j : 2 * j + 1], col[:, 2 * j + 1 : 2 * j + 2])


def left_half(rows):
    return lax.broadcasted_iota(jnp.int32, (rows, PAIR), 1) < P_SIZE


def positions(rows):
    return (
        lax.broadcasted_iota(jnp.int32, (rows, rows), 0),
        lax.broadcasted_iota(jnp.int32, (rows, rows), 1),
    )


def state_kernel(x_ref, b_ref, cum_ref, out_ref, scaled):
    rows, width = x_ref.shape
    cum = cum_ref[0]
    weight = jnp.exp(cum[rows - 1 :] - cum)
    left = left_half(rows)
    for j in range(width // PAIR):
        at = slice(j * PAIR, (j + 1) * PAIR)
        scaled[:, at] = (x_ref[:, at].astype(f32) * spread(weight, j, left)).astype(bf16)
    out_ref[0] = dot(scaled[...], b_ref[...], 0, 0).astype(bf16)


def forward_kernel(
    x_ref, gate_ref, b_ref, c_ref, cum_ref, cum_t_ref, start_ref, skip_ref, gain_ref,
    y_ref, half_ref,
):
    rows, width = x_ref.shape
    cum, cum_t = cum_ref[0], cum_t_ref[0]
    grown = jnp.exp(cum)
    left = left_half(rows)
    t, s = positions(rows)
    causal = t >= s
    scores = jnp.where(causal, dot(c_ref[...], b_ref[...], 1, 1), 0.0)
    square = jnp.zeros((rows, 1), f32)
    for j in range(width // PAIR):
        at = slice(j * PAIR, (j + 1) * PAIR)
        x = x_ref[:, at]
        inner = []
        for h in (2 * j, 2 * j + 1):
            gap = jnp.minimum(cum[:, h : h + 1] - cum_t[h : h + 1, :], 0.0)
            inner.append(dot((scores * jnp.exp(gap)).astype(bf16), x, 1, 0))
        carried = dot(c_ref[...], start_ref[0, at, :], 1, 1)
        y = jnp.where(left, inner[0], inner[1]) + spread(grown, j, left) * carried
        y_ref[:, at] = y
        v = gate_ref[:, at].astype(f32)
        gated = (y + x.astype(f32) * skip_ref[:, at]) * (v / (1.0 + jnp.exp(-v)))
        square += jnp.sum(gated * gated, axis=1, keepdims=True)
    factor = lax.rsqrt(square / width + epsilon)
    for j in range(width // PAIR):
        at = slice(j * PAIR, (j + 1) * PAIR)
        v = gate_ref[:, at].astype(f32)
        u = y_ref[:, at] + x_ref[:, at].astype(f32) * skip_ref[:, at]
        gated = u * (v / (1.0 + jnp.exp(-v)))
        half_ref[:, at] = (gated * factor * gain_ref[:, at]).astype(bf16)


def norm_back_kernel(
    x_ref, gate_ref, c_ref, cum_ref, skip_ref, gain_ref, y_ref, grad_ref,
    dy_ref, gate_grad_ref, direct_ref, scaled,
):
    rows, width = x_ref.shape
    grown = jnp.exp(cum_ref[0])
    left = left_half(rows)

    def parts(at):
        v = gate_ref[:, at].astype(f32)
        sig = 1.0 / (1.0 + jnp.exp(-v))
        u = y_ref[:, at] + x_ref[:, at].astype(f32) * skip_ref[:, at]
        return v, sig, u, u * v * sig, grad_ref[:, at] * gain_ref[:, at]

    square = jnp.zeros((rows, 1), f32)
    cross = jnp.zeros((rows, 1), f32)
    for j in range(width // PAIR):
        _, _, _, gated, dn = parts(slice(j * PAIR, (j + 1) * PAIR))
        square += jnp.sum(gated * gated, axis=1, keepdims=True)
        cross += jnp.sum(gated * dn, axis=1, keepdims=True)
    factor = lax.rsqrt(square / width + epsilon)
    back = factor * factor * (cross / width)
    for j in range(width // PAIR):
        at = slice(j * PAIR, (j + 1) * PAIR)
        v, sig, u, gated, dn = parts(at)
        dgated = factor * (dn - gated * back)
        dy = dgated * (v * sig)
        dy_ref[:, at] = dy
        gate_grad_ref[:, at] = (dgated * u * (sig * (1.0 + v * (1.0 - sig)))).astype(bf16)
        scaled[:, at] = (dy * spread(grown, j, left)).astype(bf16)
    direct_ref[0] = dot(scaled[...], c_ref[...], 0, 0).astype(bf16)


def back_kernel(
    x_ref, b_ref, c_ref, cum_ref, cum_t_ref, start_ref, end_ref, skip_ref, dy_ref,
    dx_ref, db_ref, dc_ref, decay_ref, x_scaled, dy_scaled,
):
    rows, width = x_ref.shape
    heads = cum_ref.shape[2]
    cum, cum_t = cum_ref[0], cum_t_ref[0]
    grown = jnp.exp(cum)
    fading = jnp.exp(cum[rows - 1 :] - cum)
    left = left_half(rows)
    t, s = positions(rows)
    causal = t >= s
    upper = jnp.where(t <= s, 1.0, 0.0)
    before = jnp.where(s < t, 1.0, 0.0)
    upper_half = upper.astype(bf16)
    scores = jnp.where(causal, dot(c_ref[...], b_ref[...], 1, 1), 0.0)
    lane = lax.broadcasted_iota(jnp.int32, (rows, heads), 1)
    score_grad = jnp.zeros((rows, rows), f32)
    within = jnp.zeros((rows, heads), f32)
    later = jnp.zeros((rows, heads), f32)
    earlier = jnp.zeros((rows, heads), f32)
    through = jnp.zeros((1, heads), f32)
    for j in range(width // PAIR):
        at = slice(j * PAIR, (j + 1) * PAIR)
        x = x_ref[:, at]
        dy = dy_ref[:, at]
        dy_half = dy.astype(bf16)
        start, end = start_ref[0, at, :], end_ref[0, at, :]
        dy_grown = dy * spread(grown, j, left)
        x_faded = x.astype(f32) * spread(fading, j, left)
        x_scaled[:, at] = x_faded.astype(bf16)
        dy_scaled[:, at] = dy_grown.astype(bf16)
        from_start = dy_grown * dot(c_ref[...], start, 1, 1)
        to_end = dot(b_ref[...], end, 1, 1)
        from_end = x_faded * to_end
        crossing = start.astype(f32) * end.astype(f32)
        inner = []
        for i in range(2):
            h = 2 * j + i
            mine = left if i == 0 else ~left
            own = lane == h
            gap = jnp.minimum(cum[:, h : h + 1] - cum_t[h : h + 1, :], 0.0)
            table = jnp.exp(gap)
            weights = scores * table
            pair_grad = dot(jnp.where(mine, dy_half, jnp.zeros_like(dy_half)), x, 1, 1)
            score_grad += pair_grad * table
            inner.append(dot(weights.astype(bf16), dy_half, 0, 0))
            summed = dot(upper_half, (pair_grad * weights).astype(bf16), 1, 0)
            within += jnp.where(own, jnp.sum(summed * before, axis=1, keepdims=True), 0.0)
            later += jnp.where(
                own, jnp.sum(jnp.where(mine, from_start, 0.0), axis=1, keepdims=True), 0.0
            )
            earlier += jnp.where(
                own, jnp.sum(jnp.where(mine, from_end, 0.0), axis=1, keepdims=True), 0.0
            )
            part = crossing[i * P_SIZE : (i + 1) * P_SIZE]
            total = jnp.sum(jnp.sum(part, axis=0, keepdims=True), axis=1, keepdims=True)
            through += jnp.where(own[:1], total, 0.0)
        dx = jnp.where(left, inner[0], inner[1]) + spread(fading, j, left) * to_end
        dx_ref[:, at] = (dx + dy * skip_ref[:, at]).astype(bf16)
    score_half = jnp.where(causal, score_grad, 0.0).astype(bf16)
    dc = dot(score_half, b_ref[...], 1, 0) + dot(dy_scaled[...], start_ref[0], 1, 0)
    db = dot(score_half, c_ref[...], 0, 0) + dot(x_scaled[...], end_ref[0], 1, 0)
    dc_ref[...] = dc.astype(bf16)
    db_ref[...] = db.astype(bf16)
    decay_ref[0] = (
        within
        + dot(upper, later, 1, 0, highest)
        + dot(before, earlier, 1, 0, highest)
        + jnp.exp(cum[rows - 1 :]) * through
    )


def per_device(
    ssd_input, gate_input, write_vectors, read_vectors, log_decay, skip_gain, norm_gain,
    out_weight, out_grad,
):
    rows, head_count = log_decay.shape
    groups = write_vectors.shape[1] // N
    heads = head_count // groups
    width = heads * P_SIZE
    place = lax.axis_index("seq")
    slabs = lax.axis_size("seq")

    feature = pl.BlockSpec((rows, width), lambda g: (0, g))
    vector = pl.BlockSpec((rows, N), lambda g: (0, g))
    gain = pl.BlockSpec((1, width), lambda g: (0, g))
    by_pos = pl.BlockSpec((1, rows, heads), lambda g: (g, 0, 0))
    by_head = pl.BlockSpec((1, heads, rows), lambda g: (g, 0, 0))
    state = pl.BlockSpec((1, width, N), lambda g: (g, 0, 0))
    features = (rows, groups * width)
    states = jax.ShapeDtypeStruct((groups, width, N), bf16)
    scratch = pltpu.VMEM((rows, width), bf16)

    def call(body, flops, in_specs, out_specs, out_shape, scratch_shapes=()):
        return pl.pallas_call(
            body,
            grid=(groups,),
            in_specs=in_specs,
            out_specs=out_specs,
            out_shape=out_shape,
            scratch_shapes=scratch_shapes,
            compiler_params=pltpu.CompilerParams(vmem_limit_bytes=VMEM_LIMIT),
            cost_estimate=pl.CostEstimate(
                flops=flops, bytes_accessed=8 << 20, transcendentals=1 << 20
            ),
        )

    full_grad = lax.all_gather(out_grad, "head", axis=1, tiled=True)

    t, s = positions(rows)
    cumulative = jnp.dot(jnp.where(t >= s, 1.0, 0.0), log_decay, precision=highest)
    cum = cumulative.reshape(rows, groups, heads).transpose(1, 0, 2)
    cum_t = cum.transpose(0, 2, 1)
    skip = jnp.repeat(skip_gain, P_SIZE)[None]
    gain_row = norm_gain[None]

    own_state = call(
        state_kernel, 1 << 30, [feature, vector, by_pos], state, states, [scratch]
    )(ssd_input, write_vectors, cum)

    totals = lax.all_gather(cumulative[rows - 1], "seq")
    slab = jnp.arange(slabs)
    j, i = slab[:, None, None], slab[None, :, None]
    between = (j < i) & (i < place)
    after = (place < i) & (i < j)
    log_before = jnp.sum(jnp.where(between, totals[None], 0.0), axis=1)
    log_after = jnp.sum(jnp.where(after, totals[None], 0.0), axis=1)
    share_before = jnp.where(slab[:, None] < place, jnp.exp(log_before), 0.0)
    share_after = jnp.where(slab[:, None] > place, jnp.exp(log_after), 0.0)

    def joined(own, share):
        every = lax.all_gather(own, "seq").reshape(slabs, head_count, P_SIZE, N)
        total = jnp.sum(every.astype(f32) * share[:, :, None, None], axis=0)
        return total.astype(bf16).reshape(groups, width, N)

    start_state = joined(own_state, share_before)
    ssd_out, normed_half = call(
        forward_kernel,
        4 << 30,
        [feature, feature, vector, vector, by_pos, by_head, state, gain, gain],
        [feature, feature],
        [jax.ShapeDtypeStruct(features, f32), jax.ShapeDtypeStruct(features, bf16)],
    )(ssd_input, gate_input, write_vectors, read_vectors, cum, cum_t, start_state, skip, gain_row)

    partial_out = jnp.einsum(
        "th,dh->td", normed_half, out_weight, preferred_element_type=f32
    )
    layer_out = lax.psum_scatter(
        partial_out.astype(bf16), "head", scatter_dimension=1, tiled=True
    )
    normed_all = lax.all_gather(normed_half, "seq", axis=0, tiled=True)
    grad_rows = lax.all_to_all(full_grad, "seq", split_axis=1, concat_axis=0, tiled=True)

    normed_grad = jnp.dot(full_grad, out_weight, preferred_element_type=f32)
    ssd_grad, gate_grad, direct = call(
        norm_back_kernel,
        1 << 30,
        [feature, feature, vector, by_pos, gain, gain, feature, feature],
        [feature, feature, state],
        [jax.ShapeDtypeStruct(features, f32), jax.ShapeDtypeStruct(features, bf16), states],
        [scratch],
    )(ssd_input, gate_input, read_vectors, cum, skip, gain_row, ssd_out, normed_grad)
    end_grad = joined(direct, share_after)

    vectors = jax.ShapeDtypeStruct((rows, groups * N), bf16)
    input_grad, write_grad, read_grad, decay = call(
        back_kernel,
        8 << 30,
        [feature, vector, vector, by_pos, by_head, state, state, gain, feature],
        [feature, vector, vector, by_pos],
        [
            jax.ShapeDtypeStruct(features, bf16),
            vectors,
            vectors,
            jax.ShapeDtypeStruct((groups, rows, heads), f32),
        ],
        [scratch, scratch],
    )(
        ssd_input, write_vectors, read_vectors, cum, cum_t, start_state, end_grad, skip, ssd_grad
    )
    decay_grad = decay.transpose(1, 0, 2).reshape(rows, head_count)

    weight_grad = jnp.einsum(
        "td,th->dh", grad_rows, normed_all, preferred_element_type=f32
    ).astype(bf16)
    return (layer_out, input_grad, gate_grad, write_grad, read_grad, decay_grad, weight_grad)


def solution(mesh):
    both = P("seq", "head")
    return jax.shard_map(
        per_device,
        mesh=mesh,
        in_specs=(both, both, both, both, both, P("head"), P("head"), P(None, "head"), both),
        out_specs=(both,) * 7,
        check_vma=False,
    )
```

time: 563 us -> 410 us (0.73)
  waiting for transfers between devices: 322 us -> 257 us
  matrix products: 107 us -> 50.4 us
  Pallas kernels: 0 us -> 40.8 us
  other arithmetic: 52.4 us -> 13.6 us
  local copies, waits for them, and re-layouts: 51 us -> 19 us
    reduce_scatter x2 -> x1, waiting for transfers between devices: 212 us -> 59.1 us  [per_device(): lax.psum_scatter(partial_out.astype(bf16), 'head', scatter_dimension=1, t...]
    all_to_all x0 -> x1, waiting for transfers between devices: none -> 71.3 us  [per_device(): lax.all_to_all(full_grad, 'seq', split_axis=1, concat_axis=0, tiled=True)]
    dot_general x15 -> x4, matrix products: 107 us -> 50.4 us  [the longest x1 18.7 us: per_device(): normed_grad = jnp.dot(full_grad, out_weight, preferred_element_type=f32)]
    pallas_call x0 -> x4, Pallas kernels: none -> 40.8 us  [the longest x1 20.4 us: per_device(): call(back_kernel, 8 << 30, [feature, vector, vector, by_pos, by_head, sta...]
    add x7 -> x0, other arithmetic: 27.8 us -> none  [combine(): later[0][..., None, None] * earlier[1] + later[1]]
    all_gather x2 -> x3, waiting for transfers between devices: 42 us -> 58.6 us  [the longest x2 36.7 us: joined(): every = lax.all_gather(own, 'seq').reshape(slabs, head_count, P_SIZE, N)]
    mul x6 -> x4, local copies, waits for them, and re-layouts: 12.8 us -> 0.43 us  [joined(): total = jnp.sum(every.astype(f32) * share[:, :, None, None], axis=0)]
    unnamed x91 -> x12, local copies, waits for them, and re-layouts: 16.8 us -> 8.72 us
  transfers between devices with their start and end apart: 5 -> 6, of which waited for: 4 -> 5; matrix products, arithmetic and copies ran while one was open for 26% -> 18% of each run, Pallas kernels for 0% -> 6%
where the time goes in v1:
time: 410 us
  waiting for transfers between devices  257 us (63%)
  matrix products  50.4 us (12%)
  Pallas kernels  40.8 us (10%)
  local copies, waits for them, and re-layouts  19 us (5%)
  between operations  13.9 us (3%)
  other arithmetic  13.6 us (3%)
  blocking collectives  10.2 us (2%)
  starting transfers between devices  4.98 us (1%)
    all_to_all x1, waiting for transfers between devices, per_device(): lax.all_to_all(full_grad, 'seq', split_axis=1, concat_axis=0, tiled=True)  71.3 us
    all_gather x1, waiting for transfers between devices, per_device(): full_grad = lax.all_gather(out_grad, 'head', axis=1, tiled=True)  67.1 us
    reduce_scatter x1, waiting for transfers between devices, per_device(): lax.psum_scatter(partial_out.astype(bf16), 'head', scatter_dimension=1, t...  59.1 us
    all_gather x2, waiting for transfers between devices, joined(): every = lax.all_gather(own, 'seq').reshape(slabs, head_count, P_SIZE, N)  36.7 us
    all_gather x1, waiting for transfers between devices, per_device(): normed_all = lax.all_gather(normed_half, 'seq', axis=0, tiled=True)  21.9 us
    pallas_call x1, Pallas kernels, per_device(): call(back_kernel, 8 << 30, [feature, vector, vector, by_pos, by_head, sta...  20.4 us
    dot_general x1, matrix products, per_device(): normed_grad = jnp.dot(full_grad, out_weight, preferred_element_type=f32)  18.7 us
    dot_general x1, matrix products, per_device(): jnp.einsum('th,dh->td', normed_half, out_weight, preferred_element_type=f32)  17.4 us
  transfers between devices with their start and end apart: 6, of which 5 were waited for; matrix products, arithmetic and copies ran while one was open for 18% of the time, Pallas kernels for 6%

profile of v1, /device:TPU:0, one launch (start us, length us, event | category | flops | bytes accessed | tf_op | source)
XLA Modules:
  0.0 409.6 jit_solution(10733792245769706782)
XLA Ops:
  7.2 2.3 copy.45
  9.6 0.3 fusion.2
  10.0 0.8 copy.44.cum_ref
  10.8 4.1 %shard_map.144 = bf16[2,1024,256]{2,1,0:T(8,128)(2,1)} custom-call(bf16[256,2048]{1,0:T(8,128)(2,1)} %x_ref.7, bf16[256,512]{1,0:T(8,128)(2,1)} %b_ref.5, f32[2,256,16]{2,1,0:T(8,128)} %copy.44.cum_ref), custom_call_target="tpu_custom_call" | custom-call | flops 1073741824 | bytes 8388608 | tf_op jit(solution)/shard_map/pallas_call | solution.py:237
  15.1 10.2 %all-gather.2 = f32[8,1,32]{2,1,0:T(1,128)S(1)} all-gather(f32[1,1,32]{2,1,0:T(1,128)S(1)} %bitcast.38), channel_id=1, replica_groups=mesh['seq'=8,'head'=4] {'seq'}, dimensions={0}, use_global_device_ids=true | all-gather | bytes 1152 | tf_op jit(solution)/shard_map/all_gather | solution.py:241
  25.9 0.7 broadcast_in_dim_reshape.3.skip_ref
  26.5 67.1 %all-gather.8.cloned.1.call-done = bf16[256,8192]{0,1:T(8,128)(2,1)} async-done(((bf16[256,2048]{0,1:T(8,128)(2,1)}), bf16[256,8192]{0,1:T(8,128)(2,1)}) %all-gather.8.cloned.1.call-update) | async-done | bytes 4194320 | tf_op jit(solution)/shard_map/all_gather | solution.py:228
  93.7 18.7 %fusion.10.grad_ref = f32[256,2048]{1,0:T(8,128)} fusion(bf16[256,8192]{0,1:T(8,128)(2,1)} %all-gather.8.cloned.1.call-done, bf16[8192,2048]{1,0:T(8,128)(2,1)} %param.16), kind=kOutput, calls=%fused_computation.25 | convolution fusion | flops 8589934592 | bytes 39845888 | tf_op jit(solution)/shard_map/dot_general | solution.py:274
  112.3 36.7 %all-gather.12.cloned.1.call-done = bf16[16,1024,256]{2,1,0:T(8,128)(2,1)} async-done(((bf16[2,1024,256]{2,1,0:T(8,128)(2,1)}), bf16[16,1024,256]{2,1,0:T(8,128)(2,1)}) %all-gather.12.cloned.1.call-update) | async-done | bytes 8388624 | tf_op jit(solution)/shard_map/all_gather | solution.py:252
  149.1 6.4 %fusion.1.start_ref = bf16[2,1024,256]{2,1,0:T(8,128)(2,1)} fusion(bf16[8,2,1024,256]{3,2,1,0:T(8,128)(2,1)} %bitcast.27, f32[8,2,1024]{2,1,0:T(2,128)S(1)} %mul.27), kind=kLoop, calls=%fused_computation.3 | loop fusion | flops 12058624 | bytes 9502720 | tf_op jit(solution)/shard_map/reduce_sum | solution.py:253
  155.5 9.4 %shard_map.145 = (f32[256,2048]{1,0:T(8,128)}, bf16[256,2048]{1,0:T(8,128)(2,1)}) custom-call(bf16[256,2048]{1,0:T(8,128)(2,1)} %x_ref.7, bf16[256,2048]{1,0:T(8,128)(2,1)} %gate_ref.3, bf16[256,512]{1,0:T(8,128)(2,1)} %b_ref.5, bf16[256,512]{1,0:T(8,128)(2,1)} %c_ref.5, f32[2,256,16]{2,1,0:T(8,128)} %copy.44.cum_ref, f32[2,16,256]{2,1,0:T(8,128)} %bitcast.32, ...), custom_call_target="tpu_custom_call" | custom-call | flops 4294967296 | bytes 8388608 | tf_op jit(solution)/shard_map/pallas_call | solution.py:257
  164.9 6.9 %shard_map.146 = (f32[256,2048]{1,0:T(8,128)}, bf16[256,2048]{1,0:T(8,128)(2,1)}, bf16[2,1024,256]{2,1,0:T(8,128)(2,1)}) custom-call(bf16[256,2048]{1,0:T(8,128)(2,1)} %x_ref.7, bf16[256,2048]{1,0:T(8,128)(2,1)} %gate_ref.3, bf16[256,512]{1,0:T(8,128)(2,1)} %c_ref.5, f32[2,256,16]{2,1,0:T(8,128)} %copy.44.cum_ref, ...), custom_call_target="tpu_custom_call" | custom-call | flops 1073741824 | bytes 8388608 | tf_op jit(solution)/shard_map/pallas_call | solution.py:275
  171.9 0.5 all-gather.10.cloned.1.call-update
  172.7 17.4 %convolution_convert_fusion = bf16[256,8192]{1,0:T(8,128)(2,1)} fusion(bf16[256,2048]{1,0:T(8,128)(2,1)S(1)} %copy-done.2, bf16[8192,2048]{1,0:T(8,128)(2,1)} %param.16), kind=kOutput, calls=%fused_computation.4 | convolution fusion | flops 8592031744 | bytes 38797312 | tf_op jit(solution)/shard_map/th,dh->td/dot_general | solution.py:265
  190.1 4.6 %all-to-all-start = ((bf16[256,8,1024]{0,2,1:T(8,128)(2,1)}), bf16[256,8,1024]{0,2,1:T(8,128)(2,1)}, u32[]{:S(2)}, u32[]{:S(2)}) async-start(bf16[256,8,1024]{0,2,1:T(8,128)(2,1)} %bitcast.26), calls=%async_computation.1 | async-start | bytes 8388608 | tf_op jit(solution)/shard_map/all_to_all | solution.py:272
  195.0 71.3 %all-to-all-done = bf16[256,8,1024]{0,2,1:T(8,128)(2,1)} async-done(((bf16[256,8,1024]{0,2,1:T(8,128)(2,1)}), bf16[256,8,1024]{0,2,1:T(8,128)(2,1)}, u32[]{:S(2)}, u32[]{:S(2)}) %all-to-all-start) | async-done | bytes 4194336 | tf_op jit(solution)/shard_map/all_to_all | solution.py:272
  266.3 6.4 %copy.49 = bf16[8,256,1024]{2,1,0:T(8,128)(2,1)} copy(bf16[8,256,1024]{1,2,0:T(8,128)(2,1)} %bitcast.12) | data formatting | bytes 8388608 | tf_op jit(solution)/shard_map/all_to_all | solution.py:272
  272.7 6.9 %fusion.end_ref = bf16[2,1024,256]{2,1,0:T(8,128)(2,1)} fusion(bf16[8,2,1024,256]{3,2,1,0:T(8,128)(2,1)} %bitcast.28, f32[8,2,1024]{2,1,0:T(2,128)S(1)} %mul.31), kind=kLoop, calls=%fused_computation.1 | loop fusion | flops 12058624 | bytes 9502720 | tf_op jit(solution)/shard_map/reduce_sum | solution.py:253
  279.6 20.4 %shard_map.147 = (bf16[256,2048]{1,0:T(8,128)(2,1)}, bf16[256,512]{1,0:T(8,128)(2,1)}, bf16[256,512]{1,0:T(8,128)(2,1)}, f32[2,256,16]{2,1,0:T(8,128)}) custom-call(bf16[256,2048]{1,0:T(8,128)(2,1)} %x_ref.7, bf16[256,512]{1,0:T(8,128)(2,1)} %b_ref.5, bf16[256,512]{1,0:T(8,128)(2,1)} %c_ref.5, f32[2,256,16]{2,1,0:T(8,128)} %copy.44.cum_ref, ...), custom_call_target="tpu_custom_call" | custom-call | flops 8589934592 | bytes 8388608 | tf_op jit(solution)/shard_map/pallas_call | solution.py:286
  300.0 1.7 copy.48
  301.6 21.9 %all-gather.10.cloned.1.call-done = bf16[2048,2048]{1,0:T(8,128)(2,1)} async-done(((bf16[256,2048]{1,0:T(8,128)(2,1)}), bf16[2048,2048]{1,0:T(8,128)(2,1)}) %all-gather.10.cloned.1.call-update) | async-done | bytes 8388624 | tf_op jit(solution)/shard_map/all_gather | solution.py:271
  323.5 14.0 %convert_bitcast_fusion = bf16[1024,2048]{0,1:T(8,128)(2,1)} fusion(bf16[2048,2048]{1,0:T(8,128)(2,1)} %all-gather.10.cloned.1.call-done, bf16[2048,1024]{1,0:T(8,128)(2,1)} %bitcast.29), kind=kOutput, calls=%fused_computation.5 | convolution fusion | flops 8592031744 | bytes 16777216 | tf_op jit(solution)/shard_map/td,th->dh/dot_general | solution.py:303
  337.5 6.4 %copy.50 = bf16[1024,2048]{1,0:T(8,128)(2,1)} copy(bf16[1024,2048]{0,1:T(8,128)(2,1)} %convert_bitcast_fusion) | data formatting | bytes 8388608
  344.0 59.1 %reduce-scatter.2.cloned.1.call-done = bf16[256,2048]{1,0:T(8,128)(2,1)} async-done(((bf16[256,8192]{1,0:T(8,128)(2,1)}), bf16[256,2048]{1,0:T(8,128)(2,1)}) %reduce-scatter.2.cloned.1.call-update) | async-done | bytes 1048592 | tf_op jit(solution)/shard_map/reduce_scatter | solution.py:268
  (33 shorter events, 1.4 us)
Async XLA Ops:
  7.2 2.4 copy-start
  7.2 18.6 %copy-start.4 = (f32[32]{0:T(128)S(1)}, f32[32]{0:T(128)}, u32[]{:S(2)}) copy-start(f32[32]{0:T(128)} %param.14) | copy-start | bytes 388
  7.2 86.5 %all-gather.8.cloned.1.call-start = ((), (), s32[]{:S(2)}) async-start(), calls=%async_computation.3 | async-start | bytes 5242880 | tf_op jit(solution)/shard_map/all_gather | solution.py:228
  9.5 139.5 %all-gather.12.cloned.1.call-start = ((), (), s32[]{:S(2)}) async-start(), calls=%async_computation.5 | async-start | bytes 9437184 | tf_op jit(solution)/shard_map/all_gather | solution.py:252
  9.9 102.4 %copy-start.3 = (f32[256,32]{0,1:T(8,128)}, f32[256,32]{0,1:T(8,128)S(1)}, u32[]{:S(2)}) copy-start(f32[256,32]{0,1:T(8,128)S(1)} %fusion.2) | copy-start | bytes 98308
  14.9 257.8 %all-gather.14.cloned.1.call-start = ((), (), s32[]{:S(2)}) async-start(), calls=%async_computation.6 | async-start | bytes 9437184 | tf_op jit(solution)/shard_map/all_gather | solution.py:252
  164.9 7.8 %copy-start.2 = (bf16[256,2048]{1,0:T(8,128)(2,1)S(1)}, bf16[256,2048]{1,0:T(8,128)(2,1)}, u32[]{:S(2)}) copy-start(bf16[256,2048]{1,0:T(8,128)(2,1)} %get-tuple-element.16) | copy-start | bytes 3145732
  171.9 151.7 %all-gather.10.cloned.1.call-start = ((), (), s32[]{:S(2)}) async-start(), calls=%async_computation.4 | async-start | bytes 9437184 | tf_op jit(solution)/shard_map/all_gather | solution.py:271
  172.4 230.6 %reduce-scatter.2.cloned.1.call-start = ((), (), s32[]{:S(2)}) async-start(), calls=%async_computation.2 | async-start | bytes 5242880 | tf_op jit(solution)/shard_map/reduce_scatter | solution.py:268
  190.1 76.2 %all-to-all-start = ((bf16[256,8,1024]{0,2,1:T(8,128)(2,1)}), bf16[256,8,1024]{0,2,1:T(8,128)(2,1)}, u32[]{:S(2)}, u32[]{:S(2)}) async-start(bf16[256,8,1024]{0,2,1:T(8,128)(2,1)} %bitcast.26), calls=%async_computation.1 | async-start | bytes 8388608 | tf_op jit(solution)/shard_map/all_to_all | solution.py:272
  323.5 79.5 %copy-start.1 = (f32[256,32]{0,1:T(8,128)S(1)}, f32[256,32]{0,1:T(8,128)}, u32[]{:S(2)}) copy-start(f32[256,32]{0,1:T(8,128)} %param.13) | copy-start | bytes 98308
Sparse Core Ops, SparseCore 0:
  10.2 83.4 all-gather.7
  96.1 52.9 all-gather.11
  172.0 84.0 all-gather.13
  257.8 65.7 all-gather.9
  326.3 76.7 reduce-scatter.1

commit v2 on v1

--- a/solution.py
+++ b/solution.py
@@ -226,6 +226,7 @@
         )
 
     full_grad = lax.all_gather(out_grad, "head", axis=1, tiled=True)
+    grad_rows = lax.all_to_all(full_grad, "seq", split_axis=1, concat_axis=0, tiled=True)
 
     t, s = positions(rows)
     cumulative = jnp.dot(jnp.where(t >= s, 1.0, 0.0), log_decay, precision=highest)
@@ -238,22 +239,64 @@
         state_kernel, 1 << 30, [feature, vector, by_pos], state, states, [scratch]
     )(ssd_input, write_vectors, cum)
 
-    totals = lax.all_gather(cumulative[rows - 1], "seq")
-    slab = jnp.arange(slabs)
-    j, i = slab[:, None, None], slab[None, :, None]
-    between = (j < i) & (i < place)
-    after = (place < i) & (i < j)
-    log_before = jnp.sum(jnp.where(between, totals[None], 0.0), axis=1)
-    log_after = jnp.sum(jnp.where(after, totals[None], 0.0), axis=1)
-    share_before = jnp.where(slab[:, None] < place, jnp.exp(log_before), 0.0)
-    share_after = jnp.where(slab[:, None] > place, jnp.exp(log_after), 0.0)
-
-    def joined(own, share):
-        every = lax.all_gather(own, "seq").reshape(slabs, head_count, P_SIZE, N)
-        total = jnp.sum(every.astype(f32) * share[:, :, None, None], axis=0)
-        return total.astype(bf16).reshape(groups, width, N)
-
-    start_state = joined(own_state, share_before)
+    def traded(value, step):
+        return lax.ppermute(value, "seq", [(i, i ^ step) for i in range(slabs)])
+
+    own_log = cumulative[rows - 1]
+    steps = [1 << k for k in range(1, slabs.bit_length() - 1)]
+    pair_log = traded(own_log, 1)
+    block_log = own_log + pair_log
+    block_logs = []
+    for step in steps:
+        other = traded(block_log, step)
+        block_logs.append((block_log, other))
+        block_log = block_log + other
+    odd = place & 1
+    half_heads = head_count // 2
+
+    def my_half(value):
+        return lax.dynamic_slice_in_dim(value, odd * half_heads, half_heads, 0)
+
+    def decayed(log):
+        return jnp.exp(log)[:, None, None]
+
+    def joined(own, backwards):
+        def is_later(step):
+            return ((place & step) != 0) != backwards
+
+        own = own.reshape(head_count, P_SIZE, N)
+        pair = traded(own, 1)
+        later = is_later(1)
+        mine, its = my_half(own).astype(f32), my_half(pair).astype(f32)
+        total = jnp.where(
+            later,
+            decayed(my_half(own_log)) * its + mine,
+            decayed(my_half(pair_log)) * mine + its,
+        ).astype(bf16)
+        entering = jnp.zeros_like(total)
+        entering_log = jnp.zeros((half_heads,), f32)
+        for step, (log, other_log) in zip(steps, block_logs):
+            other = traded(total, step)
+            after = is_later(step)
+            log, other_log = my_half(log), my_half(other_log)
+            mine, its = total.astype(f32), other.astype(f32)
+            entering = jnp.where(
+                after, decayed(entering_log) * its + entering.astype(f32), entering.astype(f32)
+            ).astype(bf16)
+            entering_log = jnp.where(after, entering_log + other_log, entering_log)
+            total = jnp.where(
+                after, decayed(log) * its + mine, decayed(other_log) * mine + its
+            ).astype(bf16)
+        other = traded(entering, 1)
+        whole = jnp.where(
+            odd == 0,
+            jnp.concatenate([entering, other]),
+            jnp.concatenate([other, entering]),
+        ).astype(f32)
+        whole = jnp.where(later, decayed(pair_log) * whole + pair.astype(f32), whole)
+        return whole.astype(bf16).reshape(groups, width, N)
+
+    start_state = joined(own_state, False)
     ssd_out, normed_half = call(
         forward_kernel,
         4 << 30,
@@ -269,7 +312,6 @@
         partial_out.astype(bf16), "head", scatter_dimension=1, tiled=True
     )
     normed_all = lax.all_gather(normed_half, "seq", axis=0, tiled=True)
-    grad_rows = lax.all_to_all(full_grad, "seq", split_axis=1, concat_axis=0, tiled=True)
 
     normed_grad = jnp.dot(full_grad, out_weight, preferred_element_type=f32)
     ssd_grad, gate_grad, direct = call(
@@ -280,7 +322,7 @@
         [jax.ShapeDtypeStruct(features, f32), jax.ShapeDtypeStruct(features, bf16), states],
         [scratch],
     )(ssd_input, gate_input, read_vectors, cum, skip, gain_row, ssd_out, normed_grad)
-    end_grad = joined(direct, share_after)
+    end_grad = joined(direct, True)
 
     vectors = jax.ShapeDtypeStruct((rows, groups * N), bf16)
     input_grad, write_grad, read_grad, decay = call(

time: 410 us -> 280 us (0.68)
  waiting for transfers between devices: 257 us -> 135 us
  blocking collectives: 10.2 us -> 0 us
  starting transfers between devices: 4.98 us -> 14.3 us
  other arithmetic: 13.6 us -> 6.63 us
    ppermute x0 -> x10, waiting for transfers between devices: none -> 117 us  [traded(): return lax.ppermute(value, 'seq', [(i, i ^ step) for i in range(slabs)])]
    all_to_all x1, waiting for transfers between devices: 71.3 us -> 0.01 us  [per_device(): lax.all_to_all(full_grad, 'seq', split_axis=1, concat_axis=0, tiled=True)]
    reduce_scatter x1, waiting for transfers between devices: 59.1 us -> 2.93 us  [per_device(): lax.psum_scatter(partial_out.astype(bf16), 'head', scatter_dimension=1, t...]
    all_gather x1, waiting for transfers between devices: 67.1 us -> 14.5 us  [per_device(): full_grad = lax.all_gather(out_grad, 'head', axis=1, tiled=True)]
    all_gather x2 -> x0, waiting for transfers between devices: 36.7 us -> none  [joined(): every = lax.all_gather(own, 'seq').reshape(slabs, head_count, P_SIZE, N)]
    all_gather x1, waiting for transfers between devices: 21.9 us -> 0.01 us  [per_device(): normed_all = lax.all_gather(normed_half, 'seq', axis=0, tiled=True)]
    reduce_sum x3 -> x0, other arithmetic: 13.4 us -> none  [the longest x2 13.3 us: joined(): total = jnp.sum(every.astype(f32) * share[:, :, None, None], axis=0)]
    all_gather x1 -> x0, blocking collectives: 10.2 us -> none  [per_device(): totals = lax.all_gather(cumulative[rows - 1], 'seq')]
  transfers between devices with their start and end apart: 6 -> 14, of which waited for: 5 -> 10; matrix products, arithmetic and copies ran while one was open for 18% -> 26% of each run, Pallas kernels for 6% -> 15%
where the time goes in v2:
time: 280 us; the launch traced here: 279 us
  waiting for transfers between devices  135 us (48%)
  matrix products  50.2 us (18%)
  Pallas kernels  40.7 us (15%)
  local copies, waits for them, and re-layouts  18.8 us (7%)
  starting transfers between devices  14.3 us (5%)
  between operations  13.9 us (5%)
  other arithmetic  6.63 us (2%)
    ppermute x10, waiting for transfers between devices, traded(): return lax.ppermute(value, 'seq', [(i, i ^ step) for i in range(slabs)])  117 us
    pallas_call x1, Pallas kernels, per_device(): call(back_kernel, 8 << 30, [feature, vector, vector, by_pos, by_head, sta...  20.4 us
    dot_general x1, matrix products, per_device(): normed_grad = jnp.dot(full_grad, out_weight, preferred_element_type=f32)  18.7 us
    dot_general x1, matrix products, per_device(): jnp.einsum('th,dh->td', normed_half, out_weight, preferred_element_type=f32)  16.9 us
    all_gather x1, waiting for transfers between devices, per_device(): full_grad = lax.all_gather(out_grad, 'head', axis=1, tiled=True)  14.5 us
    dot_general x1, matrix products, per_device(): jnp.einsum('td,th->dh', grad_rows, normed_all, preferred_element_type=f32)  14.3 us
    pallas_call x1, Pallas kernels, per_device(): call(forward_kernel, 4 << 30, [feature, feature, vector, vector, by_pos,...  9.35 us
    ppermute x10, starting transfers between devices, traded(): return lax.ppermute(value, 'seq', [(i, i ^ step) for i in range(slabs)])  8.89 us
  transfers between devices with their start and end apart: 14, of which 10 were waited for; matrix products, arithmetic and copies ran while one was open for 26% of the time, Pallas kernels for 15%

profile of v2, /device:TPU:0, one launch (start us, length us, event | category | flops | bytes accessed | tf_op | source)
XLA Modules:
  0.0 279.5 jit_solution(8248989567126364579)
XLA Ops:
  7.2 2.3 copy.29
  10.8 4.1 %shard_map.144 = bf16[2,1024,256]{2,1,0:T(8,128)(2,1)} custom-call(bf16[256,2048]{1,0:T(8,128)(2,1)} %x_ref.7, bf16[256,512]{1,0:T(8,128)(2,1)} %b_ref.5, f32[2,256,16]{2,1,0:T(8,128)} %copy.28.cum_ref), custom_call_target="tpu_custom_call" | custom-call | flops 1073741824 | bytes 8388608 | tf_op jit(solution)/shard_map/pallas_call | solution.py:238
  15.8 1.9 collective-permute-done
  19.3 3.0 %collective-permute-start.3 = (bf16[16,64,256]{2,1,0:T(8,128)(2,1)S(1)}, bf16[16,64,256]{2,1,0:T(8,128)(2,1)S(1)}, u32[]{:S(2)}, u32[]{:S(2)}) collective-permute-start(bf16[16,64,256]{2,1,0:T(8,128)(2,1)S(1)} %fusion.5), channel_id=1, source_target_pairs={{0,8},{4,12},{8,0},{12,4},{16,24},{20,28},{24,16},{28,20},{1,9},{5... | collective-permute-start | bytes 1572872 | tf_op jit(solution)/shard_map/ppermute | solution.py:243
  22.4 12.1 %collective-permute-done.1 = f32[32]{0:T(128)S(1)} collective-permute-done((f32[32]{0:T(128)S(1)}, f32[32]{0:T(128)S(1)}, u32[]{:S(2)}, u32[]{:S(2)}) %collective-permute-start.1) | collective-permute-done | bytes 160 | tf_op jit(solution)/shard_map/ppermute | solution.py:243
  35.0 1.8 collective-permute-start.4
  36.8 11.7 %collective-permute-done.4 = bf16[16,64,256]{2,1,0:T(8,128)(2,1)S(1)} collective-permute-done((bf16[16,64,256]{2,1,0:T(8,128)(2,1)S(1)}, bf16[16,64,256]{2,1,0:T(8,128)(2,1)S(1)}, u32[]{:S(2)}, u32[]{:S(2)}) %collective-permute-start.4) | collective-permute-done | bytes 524320 | tf_op jit(solution)/shard_map/ppermute | solution.py:243
  50.8 1.8 fusion.1
  52.6 9.4 %shard_map.145 = (f32[256,2048]{1,0:T(8,128)}, bf16[256,2048]{1,0:T(8,128)(2,1)}) custom-call(bf16[256,2048]{1,0:T(8,128)(2,1)} %x_ref.7, bf16[256,2048]{1,0:T(8,128)(2,1)} %gate_ref.3, bf16[256,512]{1,0:T(8,128)(2,1)} %b_ref.5, bf16[256,512]{1,0:T(8,128)(2,1)} %c_ref.5, f32[2,256,16]{2,1,0:T(8,128)} %copy.28.cum_ref, f32[2,16,256]{2,1,0:T(8,128)} %bitcast.35, ...), custom_call_target="tpu_custom_call" | custom-call | flops 4294967296 | bytes 8388608 | tf_op jit(solution)/shard_map/pallas_call | solution.py:300
  62.2 16.9 %convolution_convert_fusion = bf16[256,8192]{1,0:T(8,128)(2,1)} fusion(bf16[256,2048]{1,0:T(8,128)(2,1)} %get-tuple-element.16, bf16[8192,2048]{1,0:T(8,128)(2,1)} %param.16), kind=kOutput, calls=%fused_computation | convolution fusion | flops 8592031744 | bytes 38797312 | tf_op jit(solution)/shard_map/th,dh->td/dot_general | solution.py:308
  79.2 14.5 %all-gather.3.cloned.1.call-done = bf16[256,8192]{0,1:T(8,128)(2,1)} async-done(((bf16[256,2048]{0,1:T(8,128)(2,1)}), bf16[256,8192]{0,1:T(8,128)(2,1)}) %all-gather.3.cloned.1.call-update) | async-done | bytes 4194320 | tf_op jit(solution)/shard_map/all_gather | solution.py:228
  93.7 18.7 %fusion.26.grad_ref = f32[256,2048]{1,0:T(8,128)} fusion(bf16[256,8192]{0,1:T(8,128)(2,1)} %all-gather.3.cloned.1.call-done, bf16[8192,2048]{1,0:T(8,128)(2,1)} %param.16), kind=kOutput, calls=%fused_computation.62 | convolution fusion | flops 8589934592 | bytes 39845888 | tf_op jit(solution)/shard_map/dot_general | solution.py:316
  112.4 6.8 %shard_map.146 = (f32[256,2048]{1,0:T(8,128)}, bf16[256,2048]{1,0:T(8,128)(2,1)}, bf16[2,1024,256]{2,1,0:T(8,128)(2,1)}) custom-call(bf16[256,2048]{1,0:T(8,128)(2,1)} %x_ref.7, bf16[256,2048]{1,0:T(8,128)(2,1)} %gate_ref.3, bf16[256,512]{1,0:T(8,128)(2,1)} %c_ref.5, f32[2,256,16]{2,1,0:T(8,128)} %copy.28.cum_ref, ...), custom_call_target="tpu_custom_call" | custom-call | flops 1073741824 | bytes 8388608 | tf_op jit(solution)/shard_map/pallas_call | solution.py:317
  119.2 5.1 %all-to-all-start = ((bf16[256,8,1024]{0,2,1:T(8,128)(2,1)}), bf16[256,8,1024]{0,2,1:T(8,128)(2,1)}, u32[]{:S(2)}, u32[]{:S(2)}) async-start(bf16[256,8,1024]{0,2,1:T(8,128)(2,1)} %bitcast.24), calls=%async_computation.1 | async-start | bytes 8388608 | tf_op jit(solution)/shard_map/all_to_all | solution.py:229
  124.7 1.7 collective-permute-start.7
  126.4 76.2 %collective-permute-done.7 = bf16[16,64,256]{2,1,0:T(8,128)(2,1)S(1)} collective-permute-done((bf16[16,64,256]{2,1,0:T(8,128)(2,1)S(1)}, bf16[16,64,256]{2,1,0:T(8,128)(2,1)S(1)}, u32[]{:S(2)}, u32[]{:S(2)}) %collective-permute-start.7) | collective-permute-done | bytes 524320 | tf_op jit(solution)/shard_map/ppermute | solution.py:243
  204.6 12.3 %collective-permute-done.8 = bf16[16,64,256]{2,1,0:T(8,128)(2,1)S(1)} collective-permute-done((bf16[16,64,256]{2,1,0:T(8,128)(2,1)S(1)}, bf16[16,64,256]{2,1,0:T(8,128)(2,1)S(1)}, u32[]{:S(2)}, u32[]{:S(2)}) %collective-permute-start.8) | collective-permute-done | bytes 524320 | tf_op jit(solution)/shard_map/ppermute | solution.py:243
  217.3 1.9 collective-permute-done.9
  219.2 1.7 fusion.3
  220.8 20.4 %shard_map.147 = (bf16[256,2048]{1,0:T(8,128)(2,1)}, bf16[256,512]{1,0:T(8,128)(2,1)}, bf16[256,512]{1,0:T(8,128)(2,1)}, f32[2,256,16]{2,1,0:T(8,128)}) custom-call(bf16[256,2048]{1,0:T(8,128)(2,1)} %x_ref.7, bf16[256,512]{1,0:T(8,128)(2,1)} %b_ref.5, bf16[256,512]{1,0:T(8,128)(2,1)} %c_ref.5, f32[2,256,16]{2,1,0:T(8,128)} %copy.28.cum_ref, ...), custom_call_target="tpu_custom_call" | custom-call | flops 8589934592 | bytes 8388608 | tf_op jit(solution)/shard_map/pallas_call | solution.py:328
  242.9 6.4 %copy.33 = bf16[8,256,1024]{2,1,0:T(8,128)(2,1)} copy(bf16[8,256,1024]{1,2,0:T(8,128)(2,1)} %bitcast.13) | data formatting | bytes 8388608 | tf_op jit(solution)/shard_map/all_to_all | solution.py:229
  249.3 14.3 %convert_bitcast_fusion = bf16[1024,2048]{0,1:T(8,128)(2,1)} fusion(bf16[2048,2048]{1,0:T(8,128)(2,1)} %all-gather.5.cloned.1.call-done, bf16[2048,1024]{1,0:T(8,128)(2,1)} %bitcast.25), kind=kOutput, calls=%fused_computation.1 | convolution fusion | flops 8592031744 | bytes 16777216 | tf_op jit(solution)/shard_map/td,th->dh/dot_general | solution.py:345
  263.6 6.4 %copy.34 = bf16[1024,2048]{1,0:T(8,128)(2,1)} copy(bf16[1024,2048]{0,1:T(8,128)(2,1)} %convert_bitcast_fusion) | data formatting | bytes 8388608
  270.0 2.9 %reduce-scatter.2.cloned.1.call-done = bf16[256,2048]{1,0:T(8,128)(2,1)} async-done(((bf16[256,8192]{1,0:T(8,128)(2,1)}), bf16[256,2048]{1,0:T(8,128)(2,1)}) %reduce-scatter.2.cloned.1.call-update) | async-done | bytes 1048592 | tf_op jit(solution)/shard_map/reduce_scatter | solution.py:311
  (46 shorter events, 11.2 us)
Async XLA Ops:
  7.2 2.4 copy-start
  7.2 86.5 %all-gather.3.cloned.1.call-start = ((), (), s32[]{:S(2)}) async-start(), calls=%async_computation.3 | async-start | bytes 5242880 | tf_op jit(solution)/shard_map/all_gather | solution.py:228
  9.5 239.8 %all-gather.5.cloned.1.call-start = ((), (), s32[]{:S(2)}) async-start(), calls=%async_computation.4 | async-start | bytes 9437184 | tf_op jit(solution)/shard_map/all_gather | solution.py:314
  9.9 38.9 %copy-start.3 = (f32[256,32]{0,1:T(8,128)}, f32[256,32]{0,1:T(8,128)S(1)}, u32[]{:S(2)}) copy-start(f32[256,32]{0,1:T(8,128)S(1)} %fusion.16) | copy-start | bytes 98308
  10.8 38.2 %copy-start.4 = (f32[32]{0:T(128)S(1)}, f32[32]{0:T(128)}, u32[]{:S(2)}) copy-start(f32[32]{0:T(128)} %param.14) | copy-start | bytes 388
  14.9 2.9 %collective-permute-start.2 = (bf16[32,64,256]{2,1,0:T(8,128)(2,1)}, bf16[32,64,256]{2,1,0:T(8,128)(2,1)S(1)}, u32[]{:S(2)}, u32[]{:S(2)}) collective-permute-start(bf16[32,64,256]{2,1,0:T(8,128)(2,1)} %bitcast.30), channel_id=1, source_target_pairs={{0,4},{4,0},{8,12},{12,8},{16,20},{20,16},{24,28},{28,24},{1,5},{5... | collective-permute-start | bytes 3145736 | tf_op jit(solution)/shard_map/ppermute | solution.py:243
  15.5 2.1 collective-permute-start
  19.3 15.3 %collective-permute-start.3 = (bf16[16,64,256]{2,1,0:T(8,128)(2,1)S(1)}, bf16[16,64,256]{2,1,0:T(8,128)(2,1)S(1)}, u32[]{:S(2)}, u32[]{:S(2)}) collective-permute-start(bf16[16,64,256]{2,1,0:T(8,128)(2,1)S(1)} %fusion.5), channel_id=1, source_target_pairs={{0,8},{4,12},{8,0},{12,4},{16,24},{20,28},{24,16},{28,20},{1,9},{5... | collective-permute-start | bytes 1572872 | tf_op jit(solution)/shard_map/ppermute | solution.py:243
  22.3 12.3 %collective-permute-start.1 = (f32[32]{0:T(128)S(1)}, f32[32]{0:T(128)S(1)}, u32[]{:S(2)}, u32[]{:S(2)}) collective-permute-start(f32[32]{0:T(128)S(1)} %get-tuple-element.52), channel_id=1, source_target_pairs={{0,8},{4,12},{8,0},{12,4},{16,24},{20,28},{24,16},{28,20},{1,9},{5... | collective-permute-start | bytes 392 | tf_op jit(solution)/shard_map/ppermute | solution.py:243
  35.0 13.6 %collective-permute-start.4 = (bf16[16,64,256]{2,1,0:T(8,128)(2,1)S(1)}, bf16[16,64,256]{2,1,0:T(8,128)(2,1)S(1)}, u32[]{:S(2)}, u32[]{:S(2)}) collective-permute-start(bf16[16,64,256]{2,1,0:T(8,128)(2,1)S(1)} %fusion.7), channel_id=1, source_target_pairs={{0,16},{4,20},{8,24},{12,28},{16,0},{20,4},{24,8},{28,12},{1,17},{... | collective-permute-start | bytes 1572872 | tf_op jit(solution)/shard_map/ppermute | solution.py:243
  48.9 2.0 collective-permute-start.5
  62.0 211.0 %reduce-scatter.2.cloned.1.call-start = ((), (), s32[]{:S(2)}) async-start(), calls=%async_computation.2 | async-start | bytes 5242880 | tf_op jit(solution)/shard_map/reduce_scatter | solution.py:311
  119.2 5.1 %collective-permute-start.6 = (bf16[32,64,256]{2,1,0:T(8,128)(2,1)}, bf16[32,64,256]{2,1,0:T(8,128)(2,1)S(1)}, u32[]{:S(2)}, u32[]{:S(2)}) collective-permute-start(bf16[32,64,256]{2,1,0:T(8,128)(2,1)} %bitcast.32), channel_id=1, source_target_pairs={{0,4},{4,0},{8,12},{12,8},{16,20},{20,16},{24,28},{28,24},{1,5},{5... | collective-permute-start | bytes 3145736 | tf_op jit(solution)/shard_map/ppermute | solution.py:243
  119.2 5.1 %copy-start.2 = (bf16[2,1024,256]{2,1,0:T(8,128)(2,1)S(1)}, bf16[2,1024,256]{2,1,0:T(8,128)(2,1)}, u32[]{:S(2)}) copy-start(bf16[2,1024,256]{2,1,0:T(8,128)(2,1)} %get-tuple-element.18) | copy-start | bytes 3145732
  119.2 123.7 %all-to-all-start = ((bf16[256,8,1024]{0,2,1:T(8,128)(2,1)}), bf16[256,8,1024]{0,2,1:T(8,128)(2,1)}, u32[]{:S(2)}, u32[]{:S(2)}) async-start(bf16[256,8,1024]{0,2,1:T(8,128)(2,1)} %bitcast.24), calls=%async_computation.1 | async-start | bytes 8388608 | tf_op jit(solution)/shard_map/all_to_all | solution.py:229
  124.7 77.9 %collective-permute-start.7 = (bf16[16,64,256]{2,1,0:T(8,128)(2,1)S(1)}, bf16[16,64,256]{2,1,0:T(8,128)(2,1)S(1)}, u32[]{:S(2)}, u32[]{:S(2)}) collective-permute-start(bf16[16,64,256]{2,1,0:T(8,128)(2,1)S(1)} %fusion.9), channel_id=1, source_target_pairs={{0,8},{4,12},{8,0},{12,4},{16,24},{20,28},{24,16},{28,20},{1,9},{5... | collective-permute-start | bytes 1572872 | tf_op jit(solution)/shard_map/ppermute | solution.py:243
  203.1 13.8 %collective-permute-start.8 = (bf16[16,64,256]{2,1,0:T(8,128)(2,1)S(1)}, bf16[16,64,256]{2,1,0:T(8,128)(2,1)S(1)}, u32[]{:S(2)}, u32[]{:S(2)}) collective-permute-start(bf16[16,64,256]{2,1,0:T(8,128)(2,1)S(1)} %fusion.11), channel_id=1, source_target_pairs={{0,16},{4,20},{8,24},{12,28},{16,0},{20,4},{24,8},{28,12},{1,17},{... | collective-permute-start | bytes 1572872 | tf_op jit(solution)/shard_map/ppermute | solution.py:243
  217.2 2.0 collective-permute-start.9
  249.3 23.6 %copy-start.1 = (f32[256,32]{0,1:T(8,128)S(1)}, f32[256,32]{0,1:T(8,128)}, u32[]{:S(2)}) copy-start(f32[256,32]{0,1:T(8,128)} %param.13) | copy-start | bytes 98308
Sparse Core Ops, SparseCore 0:
  10.2 83.4 all-gather.2
  95.5 83.4 all-gather.4
  181.9 90.9 reduce-scatter.1

commit v3 on v2

--- a/solution.py
+++ b/solution.py
@@ -226,7 +226,6 @@
         )
 
     full_grad = lax.all_gather(out_grad, "head", axis=1, tiled=True)
-    grad_rows = lax.all_to_all(full_grad, "seq", split_axis=1, concat_axis=0, tiled=True)
 
     t, s = positions(rows)
     cumulative = jnp.dot(jnp.where(t >= s, 1.0, 0.0), log_decay, precision=highest)
@@ -311,7 +310,14 @@
     layer_out = lax.psum_scatter(
         partial_out.astype(bf16), "head", scatter_dimension=1, tiled=True
     )
-    normed_all = lax.all_gather(normed_half, "seq", axis=0, tiled=True)
+    normed_all = normed_half[None]
+    for step in [1 << k for k in reversed(range(slabs.bit_length() - 1))]:
+        other = traded(normed_all, step)
+        upper = (place & step) != 0
+        normed_all = jnp.stack(
+            [jnp.where(upper, other, normed_all), jnp.where(upper, normed_all, other)], axis=1
+        ).reshape(-1, *normed_half.shape)
+    normed_all = normed_all.reshape(-1, normed_half.shape[1])
 
     normed_grad = jnp.dot(full_grad, out_weight, preferred_element_type=f32)
     ssd_grad, gate_grad, direct = call(
@@ -323,6 +329,8 @@
         [scratch],
     )(ssd_input, gate_input, read_vectors, cum, skip, gain_row, ssd_out, normed_grad)
     end_grad = joined(direct, True)
+    full_grad, end_grad = lax.optimization_barrier((full_grad, end_grad))
+    grad_rows = lax.all_to_all(full_grad, "seq", split_axis=1, concat_axis=0, tiled=True)
 
     vectors = jax.ShapeDtypeStruct((rows, groups * N), bf16)
     input_grad, write_grad, read_grad, decay = call(

time: 280 us -> 252 us (0.900)
  waiting for transfers between devices: 135 us -> 82 us
  other arithmetic: 6.63 us -> 25.3 us
  local copies, waits for them, and re-layouts: 18.8 us -> 24 us
    ppermute x10 -> x13, waiting for transfers between devices: 117 us -> 73 us  [traded(): return lax.ppermute(value, 'seq', [(i, i ^ step) for i in range(slabs)])]
    another operation x0 -> x5, other arithmetic: none -> 15 us  [per_device(): jnp.stack([jnp.where(upper, other, normed_all), jnp.where(upper, normed_a...]
    all_gather x1, waiting for transfers between devices: 14.5 us -> 2.01 us  [per_device(): full_grad = lax.all_gather(out_grad, 'head', axis=1, tiled=True)]
    another operation x0 -> x2, local copies, waits for them, and re-layouts: none -> 10.7 us  [per_device(): jnp.stack([jnp.where(upper, other, normed_all), jnp.where(upper, normed_a...]
    all_to_all x1, waiting for transfers between devices: 0.01 us -> 6.99 us  [per_device(): lax.all_to_all(full_grad, 'seq', split_axis=1, concat_axis=0, tiled=True)]
    unnamed x12 -> x11, local copies, waits for them, and re-layouts: 8.72 us -> 3.08 us
    ppermute x10 -> x13, starting transfers between devices: 8.89 us -> 11.8 us  [traded(): return lax.ppermute(value, 'seq', [(i, i ^ step) for i in range(slabs)])]
    reduce_scatter x1, waiting for transfers between devices: 2.93 us -> 0.01 us  [per_device(): lax.psum_scatter(partial_out.astype(bf16), 'head', scatter_dimension=1, t...]
  transfers between devices with their start and end apart: 14 -> 16, of which waited for: 10 -> 11; matrix products, arithmetic and copies ran while one was open for 26% -> 38% of each run, Pallas kernels for 15% -> 16%
where the time goes in v3:
time: 252 us
  waiting for transfers between devices  82 us (33%)
  matrix products  48.6 us (19%)
  Pallas kernels  40.9 us (16%)
  other arithmetic  25.3 us (10%)
  local copies, waits for them, and re-layouts  24 us (10%)
  starting transfers between devices  16.7 us (7%)
  between operations  14.2 us (6%)
    ppermute x13, waiting for transfers between devices, traded(): return lax.ppermute(value, 'seq', [(i, i ^ step) for i in range(slabs)])  73 us
    pallas_call x1, Pallas kernels, per_device(): call(back_kernel, 8 << 30, [feature, vector, vector, by_pos, by_head, sta...  20.4 us
    dot_general x1, matrix products, per_device(): normed_grad = jnp.dot(full_grad, out_weight, preferred_element_type=f32)  17.4 us
    dot_general x1, matrix products, per_device(): jnp.einsum('th,dh->td', normed_half, out_weight, preferred_element_type=f32)  16.9 us
    another operation x5, other arithmetic, per_device(): jnp.stack([jnp.where(upper, other, normed_all), jnp.where(upper, normed_a...  15 us
    dot_general x1, matrix products, per_device(): jnp.einsum('td,th->dh', grad_rows, normed_all, preferred_element_type=f32)  14 us
    ppermute x13, starting transfers between devices, traded(): return lax.ppermute(value, 'seq', [(i, i ^ step) for i in range(slabs)])  11.8 us
    another operation x2, local copies, waits for them, and re-layouts, per_device(): jnp.stack([jnp.where(upper, other, normed_all), jnp.where(upper, normed_a...  10.7 us
  transfers between devices with their start and end apart: 16, of which 11 were waited for; matrix products, arithmetic and copies ran while one was open for 38% of the time, Pallas kernels for 16%

profile of v3, /device:TPU:0, one launch (start us, length us, event | category | flops | bytes accessed | tf_op | source)
XLA Modules:
  0.0 251.7 jit_solution(14728338790252991980)
XLA Ops:
  7.2 2.3 copy.29
  10.8 4.1 %shard_map.144 = bf16[2,1024,256]{2,1,0:T(8,128)(2,1)} custom-call(bf16[256,2048]{1,0:T(8,128)(2,1)} %x_ref.7, bf16[256,512]{1,0:T(8,128)(2,1)} %b_ref.5, f32[2,256,16]{2,1,0:T(8,128)} %copy.28.cum_ref), custom_call_target="tpu_custom_call" | custom-call | flops 1073741824 | bytes 8388608 | tf_op jit(solution)/shard_map/pallas_call | solution.py:237
  15.8 1.9 collective-permute-done
  19.3 3.0 %collective-permute-start.3 = (bf16[16,64,256]{2,1,0:T(8,128)(2,1)S(1)}, bf16[16,64,256]{2,1,0:T(8,128)(2,1)S(1)}, u32[]{:S(2)}, u32[]{:S(2)}) collective-permute-start(bf16[16,64,256]{2,1,0:T(8,128)(2,1)S(1)} %fusion.5), channel_id=1, source_target_pairs={{0,8},{4,12},{8,0},{12,4},{16,24},{20,28},{24,16},{28,20},{1,9},{5... | collective-permute-start | bytes 1572872 | tf_op jit(solution)/shard_map/ppermute | solution.py:242
  22.4 12.1 %collective-permute-done.1 = f32[32]{0:T(128)S(1)} collective-permute-done((f32[32]{0:T(128)S(1)}, f32[32]{0:T(128)S(1)}, u32[]{:S(2)}, u32[]{:S(2)}) %collective-permute-start.1) | collective-permute-done | bytes 160 | tf_op jit(solution)/shard_map/ppermute | solution.py:242
  36.8 11.7 %collective-permute-done.4 = bf16[16,64,256]{2,1,0:T(8,128)(2,1)S(1)} collective-permute-done((bf16[16,64,256]{2,1,0:T(8,128)(2,1)S(1)}, bf16[16,64,256]{2,1,0:T(8,128)(2,1)S(1)}, u32[]{:S(2)}, u32[]{:S(2)}) %collective-permute-start.4) | collective-permute-done | bytes 524320 | tf_op jit(solution)/shard_map/ppermute | solution.py:242
  52.6 9.3 %shard_map.145 = (f32[256,2048]{1,0:T(8,128)}, bf16[256,2048]{1,0:T(8,128)(2,1)}) custom-call(bf16[256,2048]{1,0:T(8,128)(2,1)} %x_ref.7, bf16[256,2048]{1,0:T(8,128)(2,1)} %gate_ref.3, bf16[256,512]{1,0:T(8,128)(2,1)} %b_ref.5, bf16[256,512]{1,0:T(8,128)(2,1)} %c_ref.5, f32[2,256,16]{2,1,0:T(8,128)} %copy.28.cum_ref, f32[2,16,256]{2,1,0:T(8,128)} %bitcast.60, ...), custom_call_target="tpu_custom_call" | custom-call | flops 4294967296 | bytes 8388608 | tf_op jit(solution)/shard_map/pallas_call | solution.py:299
  63.4 24.0 %collective-permute-done.10 = bf16[1,256,2048]{2,1,0:T(8,128)(2,1)S(1)} collective-permute-done((bf16[1,256,2048]{2,1,0:T(8,128)(2,1)}, bf16[1,256,2048]{2,1,0:T(8,128)(2,1)S(1)}, u32[]{:S(2)}, u32[]{:S(2)}) %collective-permute-start.10) | collective-permute-done | bytes 1048608 | tf_op jit(solution)/shard_map/ppermute | solution.py:242
  91.6 2.0 all-gather.2.cloned.1.call-done
  93.7 17.4 %fusion.26.grad_ref = f32[256,2048]{1,0:T(8,128)} fusion(bf16[256,8192]{0,1:T(8,128)(2,1)} %all-gather.2.cloned.1.call-done, bf16[8192,2048]{1,0:T(8,128)(2,1)} %param.16), kind=kOutput, calls=%fused_computation.71 | convolution fusion | flops 8589934592 | bytes 39845888 | tf_op jit(solution)/shard_map/dot_general | solution.py:322
  111.0 7.0 %shard_map.146 = (f32[256,2048]{1,0:T(8,128)}, bf16[256,2048]{1,0:T(8,128)(2,1)}, bf16[2,1024,256]{2,1,0:T(8,128)(2,1)}) custom-call(bf16[256,2048]{1,0:T(8,128)(2,1)} %x_ref.7, bf16[256,2048]{1,0:T(8,128)(2,1)} %gate_ref.3, bf16[256,512]{1,0:T(8,128)(2,1)} %c_ref.5, f32[2,256,16]{2,1,0:T(8,128)} %copy.28.cum_ref, ...), custom_call_target="tpu_custom_call" | custom-call | flops 1073741824 | bytes 8388608 | tf_op jit(solution)/shard_map/pallas_call | solution.py:323
  118.1 16.9 %convolution_convert_fusion = bf16[256,8192]{1,0:T(8,128)(2,1)} fusion(bf16[256,2048]{1,0:T(8,128)(2,1)} %get-tuple-element.18, bf16[8192,2048]{1,0:T(8,128)(2,1)} %param.16), kind=kOutput, calls=%fused_computation | convolution fusion | flops 8592031744 | bytes 38797312 | tf_op jit(solution)/shard_map/th,dh->td/dot_general | solution.py:307
  140.3 2.3 copy.34
  142.8 8.0 %collective-permute-done.7 = bf16[16,64,256]{2,1,0:T(8,128)(2,1)S(1)} collective-permute-done((bf16[16,64,256]{2,1,0:T(8,128)(2,1)S(1)}, bf16[16,64,256]{2,1,0:T(8,128)(2,1)S(1)}, u32[]{:S(2)}, u32[]{:S(2)}) %collective-permute-start.7) | collective-permute-done | bytes 524320 | tf_op jit(solution)/shard_map/ppermute | solution.py:242
  153.6 12.1 %collective-permute-done.8 = bf16[16,64,256]{2,1,0:T(8,128)(2,1)S(1)} collective-permute-done((bf16[16,64,256]{2,1,0:T(8,128)(2,1)S(1)}, bf16[16,64,256]{2,1,0:T(8,128)(2,1)S(1)}, u32[]{:S(2)}, u32[]{:S(2)}) %collective-permute-start.8) | collective-permute-done | bytes 524320 | tf_op jit(solution)/shard_map/ppermute | solution.py:242
  167.1 1.9 collective-permute-done.9
  170.7 4.8 %all-to-all-start = ((bf16[256,8,1024]{0,2,1:T(8,128)(2,1)}), bf16[256,8,1024]{0,2,1:T(8,128)(2,1)}, u32[]{:S(2)}, u32[]{:S(2)}) async-start(bf16[256,8,1024]{0,2,1:T(8,128)(2,1)} %bitcast.47), calls=%async_computation.1 | async-start | bytes 8388608 | tf_op jit(solution)/shard_map/all_to_all | solution.py:333
  175.5 20.4 %shard_map.147 = (bf16[256,2048]{1,0:T(8,128)(2,1)}, bf16[256,512]{1,0:T(8,128)(2,1)}, bf16[256,512]{1,0:T(8,128)(2,1)}, f32[2,256,16]{2,1,0:T(8,128)}) custom-call(bf16[256,2048]{1,0:T(8,128)(2,1)} %x_ref.7, bf16[256,512]{1,0:T(8,128)(2,1)} %b_ref.5, bf16[256,512]{1,0:T(8,128)(2,1)} %c_ref.5, f32[2,256,16]{2,1,0:T(8,128)} %copy.28.cum_ref, ...), custom_call_target="tpu_custom_call" | custom-call | flops 8589934592 | bytes 8388608 | tf_op jit(solution)/shard_map/pallas_call | solution.py:336
  197.6 5.3 %select_bitcast_fusion.1 = (bf16[4,1,256,2048]{3,2,0,1:T(8,128)(2,1)S(1)}, bf16[4,1,256,2048]{3,2,0,1:T(8,128)(2,1)}) fusion(bf16[4,256,2048]{2,1,0:T(8,128)(2,1)} %collective-permute-done.12, pred[]{:T(512)S(6)} %ne.24, bf16[2,2,256,2048]{3,2,1,0:T(8,128)(2,1)} %copy.34), kind=kLoop, calls=%fused_computation.4 | loop fusion | flops 4194304 | bytes 16777216 | tf_op jit(solution)/shard_map/stack | solution.py:317
  202.8 6.2 %pad_maximum_fusion = bf16[4,2,256,2048]{3,2,0,1:T(8,128)(2,1)} fusion(bf16[4,1,256,2048]{3,2,0,1:T(8,128)(2,1)} %get-tuple-element.30, bf16[4,1,256,2048]{3,2,0,1:T(8,128)(2,1)S(1)} %get-tuple-element.29), kind=kLoop, calls=%fused_computation.1 | loop fusion | flops 4194304 | bytes 16777216 | tf_op jit(solution)/shard_map/stack | solution.py:317
  209.0 8.4 %copy.35 = bf16[4,2,256,2048]{3,2,1,0:T(8,128)(2,1)} copy(bf16[4,2,256,2048]{3,2,0,1:T(8,128)(2,1)} %pad_maximum_fusion) | data formatting | bytes 16777216 | tf_op jit(solution)/shard_map/stack | solution.py:317
  217.4 7.0 %all-to-all-done = bf16[256,8,1024]{0,2,1:T(8,128)(2,1)} async-done(((bf16[256,8,1024]{0,2,1:T(8,128)(2,1)}), bf16[256,8,1024]{0,2,1:T(8,128)(2,1)}, u32[]{:S(2)}, u32[]{:S(2)}) %all-to-all-start) | async-done | bytes 4194336 | tf_op jit(solution)/shard_map/all_to_all | solution.py:333
  224.4 6.4 %copy.33 = bf16[8,256,1024]{2,1,0:T(8,128)(2,1)} copy(bf16[8,256,1024]{1,2,0:T(8,128)(2,1)} %bitcast.13) | data formatting | bytes 8388608 | tf_op jit(solution)/shard_map/all_to_all | solution.py:333
  230.8 14.0 %convolution_convert_fusion.1 = bf16[1024,2048]{1,0:T(8,128)(2,1)} fusion(bf16[2048,1024]{1,0:T(8,128)(2,1)} %bitcast.49, bf16[2048,2048]{1,0:T(8,128)(2,1)} %bitcast.48), kind=kOutput, calls=%fused_computation.5 | convolution fusion | flops 8592031744 | bytes 16777216 | tf_op jit(solution)/shard_map/td,th->dh/dot_general | solution.py:353
  (56 shorter events, 29.0 us)
Async XLA Ops:
  7.2 2.4 copy-start
  7.2 86.5 %all-gather.2.cloned.1.call-start = ((), (), s32[]{:S(2)}) async-start(), calls=%async_computation.3 | async-start | bytes 5242880 | tf_op jit(solution)/shard_map/all_gather | solution.py:228
  9.5 235.3 %reduce-scatter.2.cloned.1.call-start = ((), (), s32[]{:S(2)}) async-start(), calls=%async_computation.2 | async-start | bytes 5242880 | tf_op jit(solution)/shard_map/reduce_scatter | solution.py:310
  9.9 38.9 %copy-start.3 = (f32[256,32]{0,1:T(8,128)}, f32[256,32]{0,1:T(8,128)S(1)}, u32[]{:S(2)}) copy-start(f32[256,32]{0,1:T(8,128)S(1)} %fusion.16) | copy-start | bytes 98308
  10.8 38.2 %copy-start.4 = (f32[32]{0:T(128)S(1)}, f32[32]{0:T(128)}, u32[]{:S(2)}) copy-start(f32[32]{0:T(128)} %param.14) | copy-start | bytes 388
  14.9 3.0 %collective-permute-start.2 = (bf16[32,64,256]{2,1,0:T(8,128)(2,1)}, bf16[32,64,256]{2,1,0:T(8,128)(2,1)S(1)}, u32[]{:S(2)}, u32[]{:S(2)}) collective-permute-start(bf16[32,64,256]{2,1,0:T(8,128)(2,1)} %bitcast.55), channel_id=1, source_target_pairs={{0,4},{4,0},{8,12},{12,8},{16,20},{20,16},{24,28},{28,24},{1,5},{5... | collective-permute-start | bytes 3145736 | tf_op jit(solution)/shard_map/ppermute | solution.py:242
  15.5 2.1 collective-permute-start
  19.3 15.3 %collective-permute-start.3 = (bf16[16,64,256]{2,1,0:T(8,128)(2,1)S(1)}, bf16[16,64,256]{2,1,0:T(8,128)(2,1)S(1)}, u32[]{:S(2)}, u32[]{:S(2)}) collective-permute-start(bf16[16,64,256]{2,1,0:T(8,128)(2,1)S(1)} %fusion.5), channel_id=1, source_target_pairs={{0,8},{4,12},{8,0},{12,4},{16,24},{20,28},{24,16},{28,20},{1,9},{5... | collective-permute-start | bytes 1572872 | tf_op jit(solution)/shard_map/ppermute | solution.py:242
  22.3 12.3 %collective-permute-start.1 = (f32[32]{0:T(128)S(1)}, f32[32]{0:T(128)S(1)}, u32[]{:S(2)}, u32[]{:S(2)}) collective-permute-start(f32[32]{0:T(128)S(1)} %get-tuple-element.41), channel_id=1, source_target_pairs={{0,8},{4,12},{8,0},{12,4},{16,24},{20,28},{24,16},{28,20},{1,9},{5... | collective-permute-start | bytes 392 | tf_op jit(solution)/shard_map/ppermute | solution.py:242
  35.0 13.6 %collective-permute-start.4 = (bf16[16,64,256]{2,1,0:T(8,128)(2,1)S(1)}, bf16[16,64,256]{2,1,0:T(8,128)(2,1)S(1)}, u32[]{:S(2)}, u32[]{:S(2)}) collective-permute-start(bf16[16,64,256]{2,1,0:T(8,128)(2,1)S(1)} %fusion.7), channel_id=1, source_target_pairs={{0,16},{4,20},{8,24},{12,28},{16,0},{20,4},{24,8},{28,12},{1,17},{... | collective-permute-start | bytes 1572872 | tf_op jit(solution)/shard_map/ppermute | solution.py:242
  48.9 2.0 collective-permute-start.5
  61.9 25.4 %collective-permute-start.10 = (bf16[1,256,2048]{2,1,0:T(8,128)(2,1)}, bf16[1,256,2048]{2,1,0:T(8,128)(2,1)S(1)}, u32[]{:S(2)}, u32[]{:S(2)}) collective-permute-start(bf16[1,256,2048]{2,1,0:T(8,128)(2,1)} %bitcast.50), channel_id=1, source_target_pairs={{0,16},{4,20},{8,24},{12,28},{16,0},{20,4},{24,8},{28,12},{1,17},{... | collective-permute-start | bytes 3145736 | tf_op jit(solution)/shard_map/ppermute | solution.py:242
  90.2 47.8 %collective-permute-start.11 = (bf16[2,256,2048]{2,1,0:T(8,128)(2,1)}, bf16[2,256,2048]{2,1,0:T(8,128)(2,1)}, u32[]{:S(2)}, u32[]{:S(2)}) collective-permute-start(bf16[2,256,2048]{2,1,0:T(8,128)(2,1)} %maximum_bitcast_fusion), channel_id=1, source_target_pairs={{0,8},{4,12},{8,0},{12,4},{16,24},{20,28},{24,16},{28,20},{1,9},{5... | collective-permute-start | bytes 6291464 | tf_op jit(solution)/shard_map/ppermute | solution.py:242
  118.0 17.0 %collective-permute-start.6 = (bf16[32,64,256]{2,1,0:T(8,128)(2,1)}, bf16[32,64,256]{2,1,0:T(8,128)(2,1)S(1)}, u32[]{:S(2)}, u32[]{:S(2)}) collective-permute-start(bf16[32,64,256]{2,1,0:T(8,128)(2,1)} %bitcast.57), channel_id=1, source_target_pairs={{0,4},{4,0},{8,12},{12,8},{16,20},{20,16},{24,28},{28,24},{1,5},{5... | collective-permute-start | bytes 3145736 | tf_op jit(solution)/shard_map/ppermute | solution.py:242
  136.5 14.4 %collective-permute-start.7 = (bf16[16,64,256]{2,1,0:T(8,128)(2,1)S(1)}, bf16[16,64,256]{2,1,0:T(8,128)(2,1)S(1)}, u32[]{:S(2)}, u32[]{:S(2)}) collective-permute-start(bf16[16,64,256]{2,1,0:T(8,128)(2,1)S(1)} %fusion.9), channel_id=1, source_target_pairs={{0,8},{4,12},{8,0},{12,4},{16,24},{20,28},{24,16},{28,20},{1,9},{5... | collective-permute-start | bytes 1572872 | tf_op jit(solution)/shard_map/ppermute | solution.py:242
  142.6 55.0 %collective-permute-start.12 = (bf16[4,256,2048]{2,1,0:T(8,128)(2,1)}, bf16[4,256,2048]{2,1,0:T(8,128)(2,1)}, u32[]{:S(2)}, u32[]{:S(2)}) collective-permute-start(bf16[4,256,2048]{2,1,0:T(8,128)(2,1)} %bitcast.21), channel_id=1, source_target_pairs={{0,4},{4,0},{8,12},{12,8},{16,20},{20,16},{24,28},{28,24},{1,5},{5... | collective-permute-start | bytes 12582920 | tf_op jit(solution)/shard_map/ppermute | solution.py:242
  150.8 0.8 copy-start.2
  152.0 13.7 %collective-permute-start.8 = (bf16[16,64,256]{2,1,0:T(8,128)(2,1)S(1)}, bf16[16,64,256]{2,1,0:T(8,128)(2,1)S(1)}, u32[]{:S(2)}, u32[]{:S(2)}) collective-permute-start(bf16[16,64,256]{2,1,0:T(8,128)(2,1)S(1)} %fusion.11), channel_id=1, source_target_pairs={{0,16},{4,20},{8,24},{12,28},{16,0},{20,4},{24,8},{28,12},{1,17},{... | collective-permute-start | bytes 1572872 | tf_op jit(solution)/shard_map/ppermute | solution.py:242
  167.0 2.0 collective-permute-start.9
  170.7 53.7 %all-to-all-start = ((bf16[256,8,1024]{0,2,1:T(8,128)(2,1)}), bf16[256,8,1024]{0,2,1:T(8,128)(2,1)}, u32[]{:S(2)}, u32[]{:S(2)}) async-start(bf16[256,8,1024]{0,2,1:T(8,128)(2,1)} %bitcast.47), calls=%async_computation.1 | async-start | bytes 8388608 | tf_op jit(solution)/shard_map/all_to_all | solution.py:333
  230.8 14.0 %copy-start.1 = (f32[256,32]{0,1:T(8,128)S(1)}, f32[256,32]{0,1:T(8,128)}, u32[]{:S(2)}) copy-start(f32[256,32]{0,1:T(8,128)} %param.13) | copy-start | bytes 98308
Sparse Core Ops, SparseCore 0:
  10.2 83.4 all-gather.1
  135.1 75.4 reduce-scatter.1
